TPU v7x, 512 devices: a whole 4x8x8 slice. The times are simulated.
512 devices in a mesh: section: 8 (over x, core), neuron: 64 (over z, y).
Axes of the slice: x: 4, y: 8, z: 8, core: 2. Of those that a mesh axis runs over, the one named last changes fastest.
Arguments:
- features: bfloat16 [128, 65536], P('section', 'neuron'), may hold values from 0 to 16
- tiles: bfloat16 [8, 16384, 4096], P('section', 'neuron'), may hold values from -0.3125 to 0.3125
- tile_row: int32 [8, 16384], P('section'), may hold values from 0 to 1023, as said below
- tile_col: int32 [8, 16384], P('section', 'neuron'), may hold values from 0 to 15
- tile_count: int32 [8, 64], P('section'), may hold values from 128 to 256, as said below
- bias: float32 [8, 65536], P('section', 'neuron'), may hold values from -0.9 to 0
Outputs:
- activations: bfloat16 [128, 65536], P('section', 'neuron')
Inputs may be any that keep to these rules, and one draw needn't show every extreme that they name: `tile_row`: tile g of a layer belongs to shard g // 256. Among the used tiles of one shard in one layer, those reading blocks of one shard (block // 16) read at most 2 distinct blocks; in every layer some shard reads exactly 2 distinct blocks of every shard. The used tiles of a shard are its first tile_count slots; every layer has a shard with all 256 used.
All inputs are finite; a program needn't handle non-finite values.
Results may differ from a plain program's by a relative error of at most 0.02.
Values may be sent and summed in bfloat16 or wider, within the bound.
No kernel may reach another device: no remote copies, remote signals or barrier semaphores. Data moves between devices by JAX's collectives and lax.ppermute only.
A program may use at most 64 MiB of HBM per device.

v0:
```python
import jax
import jax.numpy as jnp
from jax import lax
from jax.sharding import PartitionSpec as P

BS = 64


CLAMP_TOP = 32.0


def passed_along(value, axis, steps):
    count = lax.axis_size(axis)
    first, last = (max(0, -steps), min(count, count - steps))
    return lax.ppermute(value, axis, [(source, source + steps) for source in range(first, last)])


def body(features, tiles, tile_row, tile_col, tile_count, bias):
    neuron_count = lax.axis_size("neuron")
    section_count = lax.axis_size("section")
    own_index = lax.axis_index("neuron")
    section_index = lax.axis_index("section")
    row_dev, neuron_width = features.shape
    block_size = BS
    blocks_dev = neuron_width // block_size
    tile_slots = tiles.shape[1]
    capacity = tile_slots // (2 * neuron_count)
    blocks_all = blocks_dev * neuron_count
    slot_ids = jnp.arange(tile_slots, dtype=jnp.int32)
    own_rows = lax.dynamic_slice_in_dim(tile_row[0], own_index * tile_slots, tile_slots)
    own_used = slot_ids < tile_count[0, own_index]
    matches = own_rows[:, None] == jnp.arange(blocks_all, dtype=jnp.int32)[None, :]
    need_own = (
        jnp.any(matches & own_used[:, None], axis=0)
        .astype(jnp.int32)
        .reshape(neuron_count, blocks_dev)
    )
    rank_own = jnp.cumsum(need_own, axis=1) - need_own
    rank_tile = jnp.sum(jnp.where(matches, rank_own.reshape(1, blocks_all), 0), axis=1)
    slot_of_tile = jnp.where(own_used, own_rows // blocks_dev * capacity + rank_tile, 0)
    all_rows = tile_row[0].reshape(neuron_count, tile_slots)
    all_used = slot_ids[None, :] < tile_count[0][:, None]
    local_rows = all_rows - own_index * blocks_dev
    wanted_hits = (
        local_rows[:, :, None] == jnp.arange(blocks_dev, dtype=jnp.int32)[None, None, :]
    ) & all_used[:, :, None]
    wanted = jnp.any(wanted_hits, axis=1).astype(jnp.int32)
    send_rank = jnp.cumsum(wanted, axis=1) - wanted
    picks = (wanted[:, None, :] == 1) & (
        send_rank[:, None, :] == jnp.arange(capacity, dtype=jnp.int32)[None, :, None]
    )
    picker = picks.astype(jnp.bfloat16).reshape(neuron_count * capacity, blocks_dev)
    weights = tiles[0].reshape(tile_slots, block_size, block_size)
    col_onehot = (tile_col[0][:, None] == jnp.arange(blocks_dev, dtype=jnp.int32)[None, :]).astype(
        jnp.float32
    )
    col_onehot = col_onehot * own_used[:, None].astype(jnp.float32)
    layer_bias = bias[0]

    def layer(activation):
        micro_rows = activation.shape[0]
        blocks = activation.reshape(micro_rows, blocks_dev, block_size)
        outgoing = jnp.einsum(
            "sj,rjo->sro", picker, blocks, preferred_element_type=jnp.float32
        ).astype(jnp.bfloat16)
        incoming = lax.all_to_all(outgoing, "neuron", split_axis=0, concat_axis=0, tiled=True)
        inputs = jnp.take(incoming, slot_of_tile, axis=0)
        partial_value = jnp.einsum(
            "kri,kio->kro", inputs, weights, preferred_element_type=jnp.float32
        )
        summed = jnp.einsum(
            "kc,kro->rco", col_onehot, partial_value, precision=lax.Precision.HIGHEST
        )
        totals = summed.reshape(micro_rows, neuron_width) + layer_bias
        return jnp.clip(totals, 0.0, CLAMP_TOP).astype(jnp.bfloat16)

    queue_depth = 1
    micro_rows = row_dev // queue_depth
    waiting = features.reshape(queue_depth, micro_rows, neuron_width)
    carried = jnp.zeros((micro_rows, neuron_width), jnp.bfloat16)
    total_steps = queue_depth * section_count + section_count - 1

    def advance(step_index, loop_state):
        carried, waiting = loop_state
        current = jnp.where(section_index == 0, waiting[0], carried)
        result = layer(current)
        arriving = passed_along(waiting[0], "section", -1)
        waiting = jnp.concatenate([waiting[1:], arriving[None]], axis=0)
        tail_rows = jnp.where(section_index == section_count - 1, result, waiting[queue_depth - 1])
        waiting = waiting.at[queue_depth - 1].set(tail_rows)
        carried = passed_along(result, "section", 1)
        return (carried, waiting)

    carried, waiting = lax.fori_loop(0, total_steps, advance, (carried, waiting))
    return waiting.reshape(row_dev, neuron_width)


def solution(mesh):
    in_specs = (
        P("section", "neuron"),
        P("section", "neuron", None),
        P("section", None),
        P("section", "neuron"),
        P("section", None),
        P("section", "neuron"),
    )
    out_specs = P("section", "neuron")
    return jax.shard_map(body, mesh=mesh, in_specs=in_specs, out_specs=out_specs, check_vma=False)
```

profile of v0, /device:TPU:1, one launch (start us, length us, event | category | flops | bytes accessed | tf_op | source)
XLA Modules:
  0.0 568.8 jit_solution(8099264727014039903)
XLA Ops:
  7.6 3.3 copy.21
  10.9 6.7 %copy.22 = bf16[256,64,64]{2,1,0:T(8,128)(2,1)} copy(bf16[256,64,64]{0,2,1:T(8,128)(2,1)S(1)} %bitcast.53) | data formatting | bytes 4194304
  17.6 550.6 %while.17 = (s32[]{:T(128)}, bf16[16,1024]{1,0:T(8,128)(2,1)S(1)}, bf16[1,16,1024]{2,1,0:T(8,128)(2,1)S(1)}, s32[256]{0:T(256)S(1)}, pred[]{:T(512)}, /*index=5*...) while((s32[]{:T(128)}, bf16[16,1024]{1,0:T(8,128)(2,1)S(1)}, ...), condition=%wide.region_6.7_spmd.clone, body=%wide.region_5.6_spmd.clone.sunk | while | flops 88573184 | bytes 9254135 | solution.py:94
  17.6 8.8 %collective-permute-start = (bf16[16,1024]{1,0:T(8,128)(2,1)S(1)}, bf16[16,1024]{1,0:T(8,128)(2,1)S(1)}, u32[]{:S(2)}, u32[]{:S(2)}) collective-permute-start(bf16[16,1024]{1,0:T(8,128)(2,1)S(1)} %bitcast.55), channel_id=1, source_target_pairs={{64,0},{128,64},{192,128},{256,192},{320,256},{384,320},{448,384},... | collective-permute-start | bytes 98312 | tf_op jit(solution)/shard_map/while/body/eval_jaxpr/ppermute | solution.py:15
  28.4 10.9 %all-to-all-start = ((bf16[64,2,1024]{2,1,0:T(2,128)(2,1)}), bf16[64,2,1024]{2,1,0:T(2,128)(2,1)S(1)}, u32[]{:S(2)}, u32[]{:S(2)}) async-start(bf16[64,2,1024]{2,1,0:T(2,128)(2,1)} %reshape.196), calls=%async_computation | async-start | bytes 524288 | tf_op jit(solution)/shard_map/while/body/eval_jaxpr/all_to_all | solution.py:66
  39.4 14.1 %all-to-all-done = bf16[64,2,1024]{2,1,0:T(2,128)(2,1)S(1)} async-done(((bf16[64,2,1024]{2,1,0:T(2,128)(2,1)}), bf16[64,2,1024]{2,1,0:T(2,128)(2,1)S(1)}, u32[]{:S(2)}, u32[]{:S(2)}) %all-to-all-start) | async-done | bytes 262176 | tf_op jit(solution)/shard_map/while/body/eval_jaxpr/all_to_all | solution.py:66
  54.7 3.5 fusion.48
  60.0 4.7 collective-permute-start.1
  69.7 4.6 all-to-all-start
  74.3 13.2 %all-to-all-done = bf16[64,2,1024]{2,1,0:T(2,128)(2,1)S(1)} async-done(((bf16[64,2,1024]{2,1,0:T(2,128)(2,1)}), bf16[64,2,1024]{2,1,0:T(2,128)(2,1)S(1)}, u32[]{:S(2)}, u32[]{:S(2)}) %all-to-all-start) | async-done | bytes 262176 | tf_op jit(solution)/shard_map/while/body/eval_jaxpr/all_to_all | solution.py:66
  88.7 3.5 fusion.48
  94.1 6.5 %collective-permute-start.1 = (bf16[16,1024]{1,0:T(8,128)(2,1)S(1)}, bf16[16,1024]{1,0:T(8,128)(2,1)S(1)}, u32[]{:S(2)}, u32[]{:S(2)}) collective-permute-start(bf16[16,1024]{1,0:T(8,128)(2,1)S(1)} %get-tuple-element.366), channel_id=1, source_target_pairs={{0,64},{64,128},{128,192},{192,256},{256,320},{320,384},{384,448},... | collective-permute-start | bytes 98312 | tf_op jit(solution)/shard_map/while/body/eval_jaxpr/ppermute | solution.py:15
  105.5 4.6 all-to-all-start
  110.2 12.4 %all-to-all-done = bf16[64,2,1024]{2,1,0:T(2,128)(2,1)S(1)} async-done(((bf16[64,2,1024]{2,1,0:T(2,128)(2,1)}), bf16[64,2,1024]{2,1,0:T(2,128)(2,1)S(1)}, u32[]{:S(2)}, u32[]{:S(2)}) %all-to-all-start) | async-done | bytes 262176 | tf_op jit(solution)/shard_map/while/body/eval_jaxpr/all_to_all | solution.py:66
  123.8 3.5 fusion.48
  129.1 7.4 %collective-permute-start.1 = (bf16[16,1024]{1,0:T(8,128)(2,1)S(1)}, bf16[16,1024]{1,0:T(8,128)(2,1)S(1)}, u32[]{:S(2)}, u32[]{:S(2)}) collective-permute-start(bf16[16,1024]{1,0:T(8,128)(2,1)S(1)} %get-tuple-element.366), channel_id=1, source_target_pairs={{0,64},{64,128},{128,192},{192,256},{256,320},{320,384},{384,448},... | collective-permute-start | bytes 98312 | tf_op jit(solution)/shard_map/while/body/eval_jaxpr/ppermute | solution.py:15
  141.4 4.6 all-to-all-start
  146.1 12.4 %all-to-all-done = bf16[64,2,1024]{2,1,0:T(2,128)(2,1)S(1)} async-done(((bf16[64,2,1024]{2,1,0:T(2,128)(2,1)}), bf16[64,2,1024]{2,1,0:T(2,128)(2,1)S(1)}, u32[]{:S(2)}, u32[]{:S(2)}) %all-to-all-start) | async-done | bytes 262176 | tf_op jit(solution)/shard_map/while/body/eval_jaxpr/all_to_all | solution.py:66
  159.7 3.5 fusion.48
  165.0 7.4 %collective-permute-start.1 = (bf16[16,1024]{1,0:T(8,128)(2,1)S(1)}, bf16[16,1024]{1,0:T(8,128)(2,1)S(1)}, u32[]{:S(2)}, u32[]{:S(2)}) collective-permute-start(bf16[16,1024]{1,0:T(8,128)(2,1)S(1)} %get-tuple-element.366), channel_id=1, source_target_pairs={{0,64},{64,128},{128,192},{192,256},{256,320},{320,384},{384,448},... | collective-permute-start | bytes 98312 | tf_op jit(solution)/shard_map/while/body/eval_jaxpr/ppermute | solution.py:15
  177.3 4.6 all-to-all-start
  182.0 12.4 %all-to-all-done = bf16[64,2,1024]{2,1,0:T(2,128)(2,1)S(1)} async-done(((bf16[64,2,1024]{2,1,0:T(2,128)(2,1)}), bf16[64,2,1024]{2,1,0:T(2,128)(2,1)S(1)}, u32[]{:S(2)}, u32[]{:S(2)}) %all-to-all-start) | async-done | bytes 262176 | tf_op jit(solution)/shard_map/while/body/eval_jaxpr/all_to_all | solution.py:66
  195.6 3.5 fusion.48
  200.9 7.4 %collective-permute-start.1 = (bf16[16,1024]{1,0:T(8,128)(2,1)S(1)}, bf16[16,1024]{1,0:T(8,128)(2,1)S(1)}, u32[]{:S(2)}, u32[]{:S(2)}) collective-permute-start(bf16[16,1024]{1,0:T(8,128)(2,1)S(1)} %get-tuple-element.366), channel_id=1, source_target_pairs={{0,64},{64,128},{128,192},{192,256},{256,320},{320,384},{384,448},... | collective-permute-start | bytes 98312 | tf_op jit(solution)/shard_map/while/body/eval_jaxpr/ppermute | solution.py:15
  213.2 4.6 all-to-all-start
  217.9 12.4 %all-to-all-done = bf16[64,2,1024]{2,1,0:T(2,128)(2,1)S(1)} async-done(((bf16[64,2,1024]{2,1,0:T(2,128)(2,1)}), bf16[64,2,1024]{2,1,0:T(2,128)(2,1)S(1)}, u32[]{:S(2)}, u32[]{:S(2)}) %all-to-all-start) | async-done | bytes 262176 | tf_op jit(solution)/shard_map/while/body/eval_jaxpr/all_to_all | solution.py:66
  231.5 3.5 fusion.48
  236.8 7.4 %collective-permute-start.1 = (bf16[16,1024]{1,0:T(8,128)(2,1)S(1)}, bf16[16,1024]{1,0:T(8,128)(2,1)S(1)}, u32[]{:S(2)}, u32[]{:S(2)}) collective-permute-start(bf16[16,1024]{1,0:T(8,128)(2,1)S(1)} %get-tuple-element.366), channel_id=1, source_target_pairs={{0,64},{64,128},{128,192},{192,256},{256,320},{320,384},{384,448},... | collective-permute-start | bytes 98312 | tf_op jit(solution)/shard_map/while/body/eval_jaxpr/ppermute | solution.py:15
  249.1 4.6 all-to-all-start
  253.8 12.4 %all-to-all-done = bf16[64,2,1024]{2,1,0:T(2,128)(2,1)S(1)} async-done(((bf16[64,2,1024]{2,1,0:T(2,128)(2,1)}), bf16[64,2,1024]{2,1,0:T(2,128)(2,1)S(1)}, u32[]{:S(2)}, u32[]{:S(2)}) %all-to-all-start) | async-done | bytes 262176 | tf_op jit(solution)/shard_map/while/body/eval_jaxpr/all_to_all | solution.py:66
  267.4 3.5 fusion.48
  272.7 7.4 %collective-permute-start.1 = (bf16[16,1024]{1,0:T(8,128)(2,1)S(1)}, bf16[16,1024]{1,0:T(8,128)(2,1)S(1)}, u32[]{:S(2)}, u32[]{:S(2)}) collective-permute-start(bf16[16,1024]{1,0:T(8,128)(2,1)S(1)} %get-tuple-element.366), channel_id=1, source_target_pairs={{0,64},{64,128},{128,192},{192,256},{256,320},{320,384},{384,448},... | collective-permute-start | bytes 98312 | tf_op jit(solution)/shard_map/while/body/eval_jaxpr/ppermute | solution.py:15
  285.0 4.6 all-to-all-start
  289.7 12.4 %all-to-all-done = bf16[64,2,1024]{2,1,0:T(2,128)(2,1)S(1)} async-done(((bf16[64,2,1024]{2,1,0:T(2,128)(2,1)}), bf16[64,2,1024]{2,1,0:T(2,128)(2,1)S(1)}, u32[]{:S(2)}, u32[]{:S(2)}) %all-to-all-start) | async-done | bytes 262176 | tf_op jit(solution)/shard_map/while/body/eval_jaxpr/all_to_all | solution.py:66
  303.3 3.5 fusion.48
  308.6 7.4 %collective-permute-start.1 = (bf16[16,1024]{1,0:T(8,128)(2,1)S(1)}, bf16[16,1024]{1,0:T(8,128)(2,1)S(1)}, u32[]{:S(2)}, u32[]{:S(2)}) collective-permute-start(bf16[16,1024]{1,0:T(8,128)(2,1)S(1)} %get-tuple-element.366), channel_id=1, source_target_pairs={{0,64},{64,128},{128,192},{192,256},{256,320},{320,384},{384,448},... | collective-permute-start | bytes 98312 | tf_op jit(solution)/shard_map/while/body/eval_jaxpr/ppermute | solution.py:15
  320.9 4.6 all-to-all-start
  325.6 12.4 %all-to-all-done = bf16[64,2,1024]{2,1,0:T(2,128)(2,1)S(1)} async-done(((bf16[64,2,1024]{2,1,0:T(2,128)(2,1)}), bf16[64,2,1024]{2,1,0:T(2,128)(2,1)S(1)}, u32[]{:S(2)}, u32[]{:S(2)}) %all-to-all-start) | async-done | bytes 262176 | tf_op jit(solution)/shard_map/while/body/eval_jaxpr/all_to_all | solution.py:66
  339.2 3.5 fusion.48
  344.5 7.4 %collective-permute-start.1 = (bf16[16,1024]{1,0:T(8,128)(2,1)S(1)}, bf16[16,1024]{1,0:T(8,128)(2,1)S(1)}, u32[]{:S(2)}, u32[]{:S(2)}) collective-permute-start(bf16[16,1024]{1,0:T(8,128)(2,1)S(1)} %get-tuple-element.366), channel_id=1, source_target_pairs={{0,64},{64,128},{128,192},{192,256},{256,320},{320,384},{384,448},... | collective-permute-start | bytes 98312 | tf_op jit(solution)/shard_map/while/body/eval_jaxpr/ppermute | solution.py:15
  356.8 4.6 all-to-all-start
  361.4 12.4 %all-to-all-done = bf16[64,2,1024]{2,1,0:T(2,128)(2,1)S(1)} async-done(((bf16[64,2,1024]{2,1,0:T(2,128)(2,1)}), bf16[64,2,1024]{2,1,0:T(2,128)(2,1)S(1)}, u32[]{:S(2)}, u32[]{:S(2)}) %all-to-all-start) | async-done | bytes 262176 | tf_op jit(solution)/shard_map/while/body/eval_jaxpr/all_to_all | solution.py:66
  375.0 3.5 fusion.48
  380.4 7.4 %collective-permute-start.1 = (bf16[16,1024]{1,0:T(8,128)(2,1)S(1)}, bf16[16,1024]{1,0:T(8,128)(2,1)S(1)}, u32[]{:S(2)}, u32[]{:S(2)}) collective-permute-start(bf16[16,1024]{1,0:T(8,128)(2,1)S(1)} %get-tuple-element.366), channel_id=1, source_target_pairs={{0,64},{64,128},{128,192},{192,256},{256,320},{320,384},{384,448},... | collective-permute-start | bytes 98312 | tf_op jit(solution)/shard_map/while/body/eval_jaxpr/ppermute | solution.py:15
  392.7 4.6 all-to-all-start
  397.3 12.4 %all-to-all-done = bf16[64,2,1024]{2,1,0:T(2,128)(2,1)S(1)} async-done(((bf16[64,2,1024]{2,1,0:T(2,128)(2,1)}), bf16[64,2,1024]{2,1,0:T(2,128)(2,1)S(1)}, u32[]{:S(2)}, u32[]{:S(2)}) %all-to-all-start) | async-done | bytes 262176 | tf_op jit(solution)/shard_map/while/body/eval_jaxpr/all_to_all | solution.py:66
  410.9 3.5 fusion.48
  416.3 7.4 %collective-permute-start.1 = (bf16[16,1024]{1,0:T(8,128)(2,1)S(1)}, bf16[16,1024]{1,0:T(8,128)(2,1)S(1)}, u32[]{:S(2)}, u32[]{:S(2)}) collective-permute-start(bf16[16,1024]{1,0:T(8,128)(2,1)S(1)} %get-tuple-element.366), channel_id=1, source_target_pairs={{0,64},{64,128},{128,192},{192,256},{256,320},{320,384},{384,448},... | collective-permute-start | bytes 98312 | tf_op jit(solution)/shard_map/while/body/eval_jaxpr/ppermute | solution.py:15
  428.6 4.6 all-to-all-start
  433.2 12.4 %all-to-all-done = bf16[64,2,1024]{2,1,0:T(2,128)(2,1)S(1)} async-done(((bf16[64,2,1024]{2,1,0:T(2,128)(2,1)}), bf16[64,2,1024]{2,1,0:T(2,128)(2,1)S(1)}, u32[]{:S(2)}, u32[]{:S(2)}) %all-to-all-start) | async-done | bytes 262176 | tf_op jit(solution)/shard_map/while/body/eval_jaxpr/all_to_all | solution.py:66
  446.8 3.5 fusion.48
  452.2 7.4 %collective-permute-start.1 = (bf16[16,1024]{1,0:T(8,128)(2,1)S(1)}, bf16[16,1024]{1,0:T(8,128)(2,1)S(1)}, u32[]{:S(2)}, u32[]{:S(2)}) collective-permute-start(bf16[16,1024]{1,0:T(8,128)(2,1)S(1)} %get-tuple-element.366), channel_id=1, source_target_pairs={{0,64},{64,128},{128,192},{192,256},{256,320},{320,384},{384,448},... | collective-permute-start | bytes 98312 | tf_op jit(solution)/shard_map/while/body/eval_jaxpr/ppermute | solution.py:15
  464.4 4.6 all-to-all-start
  469.1 12.4 %all-to-all-done = bf16[64,2,1024]{2,1,0:T(2,128)(2,1)S(1)} async-done(((bf16[64,2,1024]{2,1,0:T(2,128)(2,1)}), bf16[64,2,1024]{2,1,0:T(2,128)(2,1)S(1)}, u32[]{:S(2)}, u32[]{:S(2)}) %all-to-all-start) | async-done | bytes 262176 | tf_op jit(solution)/shard_map/while/body/eval_jaxpr/all_to_all | solution.py:66
  482.7 3.5 fusion.48
  488.0 7.4 %collective-permute-start.1 = (bf16[16,1024]{1,0:T(8,128)(2,1)S(1)}, bf16[16,1024]{1,0:T(8,128)(2,1)S(1)}, u32[]{:S(2)}, u32[]{:S(2)}) collective-permute-start(bf16[16,1024]{1,0:T(8,128)(2,1)S(1)} %get-tuple-element.366), channel_id=1, source_target_pairs={{0,64},{64,128},{128,192},{192,256},{256,320},{320,384},{384,448},... | collective-permute-start | bytes 98312 | tf_op jit(solution)/shard_map/while/body/eval_jaxpr/ppermute | solution.py:15
  500.3 4.6 all-to-all-start
  505.0 12.4 %all-to-all-done = bf16[64,2,1024]{2,1,0:T(2,128)(2,1)S(1)} async-done(((bf16[64,2,1024]{2,1,0:T(2,128)(2,1)}), bf16[64,2,1024]{2,1,0:T(2,128)(2,1)S(1)}, u32[]{:S(2)}, u32[]{:S(2)}) %all-to-all-start) | async-done | bytes 262176 | tf_op jit(solution)/shard_map/while/body/eval_jaxpr/all_to_all | solution.py:66
  518.6 3.5 fusion.48
  523.9 7.4 %collective-permute-start.1 = (bf16[16,1024]{1,0:T(8,128)(2,1)S(1)}, bf16[16,1024]{1,0:T(8,128)(2,1)S(1)}, u32[]{:S(2)}, u32[]{:S(2)}) collective-permute-start(bf16[16,1024]{1,0:T(8,128)(2,1)S(1)} %get-tuple-element.366), channel_id=1, source_target_pairs={{0,64},{64,128},{128,192},{192,256},{256,320},{320,384},{384,448},... | collective-permute-start | bytes 98312 | tf_op jit(solution)/shard_map/while/body/eval_jaxpr/ppermute | solution.py:15
  536.2 4.6 all-to-all-start
  540.9 12.4 %all-to-all-done = bf16[64,2,1024]{2,1,0:T(2,128)(2,1)S(1)} async-done(((bf16[64,2,1024]{2,1,0:T(2,128)(2,1)}), bf16[64,2,1024]{2,1,0:T(2,128)(2,1)S(1)}, u32[]{:S(2)}, u32[]{:S(2)}) %all-to-all-start) | async-done | bytes 262176 | tf_op jit(solution)/shard_map/while/body/eval_jaxpr/all_to_all | solution.py:66
  554.5 3.5 fusion.48
  559.8 7.4 %collective-permute-start.1 = (bf16[16,1024]{1,0:T(8,128)(2,1)S(1)}, bf16[16,1024]{1,0:T(8,128)(2,1)S(1)}, u32[]{:S(2)}, u32[]{:S(2)}) collective-permute-start(bf16[16,1024]{1,0:T(8,128)(2,1)S(1)} %get-tuple-element.366), channel_id=1, source_target_pairs={{0,64},{64,128},{128,192},{192,256},{256,320},{320,384},{384,448},... | collective-permute-start | bytes 98312 | tf_op jit(solution)/shard_map/while/body/eval_jaxpr/ppermute | solution.py:15
  (313 shorter events, 125.2 us)
Async XLA Ops:
  10.9 6.7 %copy-start.1 = (bf16[16,1024]{1,0:T(8,128)(2,1)S(1)}, bf16[16,1024]{1,0:T(8,128)(2,1)}, u32[]{:S(2)}) copy-start(bf16[16,1024]{1,0:T(8,128)(2,1)} %param.10) | copy-start | bytes 98308
  10.9 6.7 %copy-start.2 = (f32[1,1024]{1,0:T(1,128)S(1)}, f32[1,1024]{1,0:T(1,128)}, u32[]{:S(2)}) copy-start(f32[1,1024]{1,0:T(1,128)} %param.15) | copy-start | bytes 12292
  10.9 6.7 %copy-start.3 = (s32[1,256]{1,0:T(1,128)S(1)}, s32[1,256]{1,0:T(1,128)}, u32[]{:S(2)}) copy-start(s32[1,256]{1,0:T(1,128)} %param.13) | copy-start | bytes 3076
  17.6 42.4 %collective-permute-start = (bf16[16,1024]{1,0:T(8,128)(2,1)S(1)}, bf16[16,1024]{1,0:T(8,128)(2,1)S(1)}, u32[]{:S(2)}, u32[]{:S(2)}) collective-permute-start(bf16[16,1024]{1,0:T(8,128)(2,1)S(1)} %bitcast.55), channel_id=1, source_target_pairs={{64,0},{128,64},{192,128},{256,192},{320,256},{384,320},{448,384},... | collective-permute-start | bytes 98312 | tf_op jit(solution)/shard_map/while/body/eval_jaxpr/ppermute | solution.py:15
  28.4 25.1 %all-to-all-start = ((bf16[64,2,1024]{2,1,0:T(2,128)(2,1)}), bf16[64,2,1024]{2,1,0:T(2,128)(2,1)S(1)}, u32[]{:S(2)}, u32[]{:S(2)}) async-start(bf16[64,2,1024]{2,1,0:T(2,128)(2,1)} %reshape.196), calls=%async_computation | async-start | bytes 524288 | tf_op jit(solution)/shard_map/while/body/eval_jaxpr/all_to_all | solution.py:66
  60.0 5.7 collective-permute-start.1
  65.7 28.3 %collective-permute-start = (bf16[16,1024]{1,0:T(8,128)(2,1)S(1)}, bf16[16,1024]{1,0:T(8,128)(2,1)S(1)}, u32[]{:S(2)}, u32[]{:S(2)}) collective-permute-start(bf16[16,1024]{1,0:T(8,128)(2,1)S(1)} %bitcast.55), channel_id=1, source_target_pairs={{64,0},{128,64},{192,128},{256,192},{320,256},{384,320},{448,384},... | collective-permute-start | bytes 98312 | tf_op jit(solution)/shard_map/while/body/eval_jaxpr/ppermute | solution.py:15
  69.7 17.9 %all-to-all-start = ((bf16[64,2,1024]{2,1,0:T(2,128)(2,1)}), bf16[64,2,1024]{2,1,0:T(2,128)(2,1)S(1)}, u32[]{:S(2)}, u32[]{:S(2)}) async-start(bf16[64,2,1024]{2,1,0:T(2,128)(2,1)} %reshape.196), calls=%async_computation | async-start | bytes 524288 | tf_op jit(solution)/shard_map/while/body/eval_jaxpr/all_to_all | solution.py:66
  94.1 7.5 %collective-permute-start.1 = (bf16[16,1024]{1,0:T(8,128)(2,1)S(1)}, bf16[16,1024]{1,0:T(8,128)(2,1)S(1)}, u32[]{:S(2)}, u32[]{:S(2)}) collective-permute-start(bf16[16,1024]{1,0:T(8,128)(2,1)S(1)} %get-tuple-element.366), channel_id=1, source_target_pairs={{0,64},{64,128},{128,192},{192,256},{256,320},{320,384},{384,448},... | collective-permute-start | bytes 98312 | tf_op jit(solution)/shard_map/while/body/eval_jaxpr/ppermute | solution.py:15
  101.6 27.5 %collective-permute-start = (bf16[16,1024]{1,0:T(8,128)(2,1)S(1)}, bf16[16,1024]{1,0:T(8,128)(2,1)S(1)}, u32[]{:S(2)}, u32[]{:S(2)}) collective-permute-start(bf16[16,1024]{1,0:T(8,128)(2,1)S(1)} %bitcast.55), channel_id=1, source_target_pairs={{64,0},{128,64},{192,128},{256,192},{320,256},{384,320},{448,384},... | collective-permute-start | bytes 98312 | tf_op jit(solution)/shard_map/while/body/eval_jaxpr/ppermute | solution.py:15
  105.5 17.1 %all-to-all-start = ((bf16[64,2,1024]{2,1,0:T(2,128)(2,1)}), bf16[64,2,1024]{2,1,0:T(2,128)(2,1)S(1)}, u32[]{:S(2)}, u32[]{:S(2)}) async-start(bf16[64,2,1024]{2,1,0:T(2,128)(2,1)} %reshape.196), calls=%async_computation | async-start | bytes 524288 | tf_op jit(solution)/shard_map/while/body/eval_jaxpr/all_to_all | solution.py:66
  129.1 8.4 %collective-permute-start.1 = (bf16[16,1024]{1,0:T(8,128)(2,1)S(1)}, bf16[16,1024]{1,0:T(8,128)(2,1)S(1)}, u32[]{:S(2)}, u32[]{:S(2)}) collective-permute-start(bf16[16,1024]{1,0:T(8,128)(2,1)S(1)} %get-tuple-element.366), channel_id=1, source_target_pairs={{0,64},{64,128},{128,192},{192,256},{256,320},{320,384},{384,448},... | collective-permute-start | bytes 98312 | tf_op jit(solution)/shard_map/while/body/eval_jaxpr/ppermute | solution.py:15
  137.5 27.5 %collective-permute-start = (bf16[16,1024]{1,0:T(8,128)(2,1)S(1)}, bf16[16,1024]{1,0:T(8,128)(2,1)S(1)}, u32[]{:S(2)}, u32[]{:S(2)}) collective-permute-start(bf16[16,1024]{1,0:T(8,128)(2,1)S(1)} %bitcast.55), channel_id=1, source_target_pairs={{64,0},{128,64},{192,128},{256,192},{320,256},{384,320},{448,384},... | collective-permute-start | bytes 98312 | tf_op jit(solution)/shard_map/while/body/eval_jaxpr/ppermute | solution.py:15
  141.4 17.1 %all-to-all-start = ((bf16[64,2,1024]{2,1,0:T(2,128)(2,1)}), bf16[64,2,1024]{2,1,0:T(2,128)(2,1)S(1)}, u32[]{:S(2)}, u32[]{:S(2)}) async-start(bf16[64,2,1024]{2,1,0:T(2,128)(2,1)} %reshape.196), calls=%async_computation | async-start | bytes 524288 | tf_op jit(solution)/shard_map/while/body/eval_jaxpr/all_to_all | solution.py:66
  165.0 8.4 %collective-permute-start.1 = (bf16[16,1024]{1,0:T(8,128)(2,1)S(1)}, bf16[16,1024]{1,0:T(8,128)(2,1)S(1)}, u32[]{:S(2)}, u32[]{:S(2)}) collective-permute-start(bf16[16,1024]{1,0:T(8,128)(2,1)S(1)} %get-tuple-element.366), channel_id=1, source_target_pairs={{0,64},{64,128},{128,192},{192,256},{256,320},{320,384},{384,448},... | collective-permute-start | bytes 98312 | tf_op jit(solution)/shard_map/while/body/eval_jaxpr/ppermute | solution.py:15
  173.4 27.5 %collective-permute-start = (bf16[16,1024]{1,0:T(8,128)(2,1)S(1)}, bf16[16,1024]{1,0:T(8,128)(2,1)S(1)}, u32[]{:S(2)}, u32[]{:S(2)}) collective-permute-start(bf16[16,1024]{1,0:T(8,128)(2,1)S(1)} %bitcast.55), channel_id=1, source_target_pairs={{64,0},{128,64},{192,128},{256,192},{320,256},{384,320},{448,384},... | collective-permute-start | bytes 98312 | tf_op jit(solution)/shard_map/while/body/eval_jaxpr/ppermute | solution.py:15
  177.3 17.1 %all-to-all-start = ((bf16[64,2,1024]{2,1,0:T(2,128)(2,1)}), bf16[64,2,1024]{2,1,0:T(2,128)(2,1)S(1)}, u32[]{:S(2)}, u32[]{:S(2)}) async-start(bf16[64,2,1024]{2,1,0:T(2,128)(2,1)} %reshape.196), calls=%async_computation | async-start | bytes 524288 | tf_op jit(solution)/shard_map/while/body/eval_jaxpr/all_to_all | solution.py:66
  200.9 8.4 %collective-permute-start.1 = (bf16[16,1024]{1,0:T(8,128)(2,1)S(1)}, bf16[16,1024]{1,0:T(8,128)(2,1)S(1)}, u32[]{:S(2)}, u32[]{:S(2)}) collective-permute-start(bf16[16,1024]{1,0:T(8,128)(2,1)S(1)} %get-tuple-element.366), channel_id=1, source_target_pairs={{0,64},{64,128},{128,192},{192,256},{256,320},{320,384},{384,448},... | collective-permute-start | bytes 98312 | tf_op jit(solution)/shard_map/while/body/eval_jaxpr/ppermute | solution.py:15
  209.3 27.5 %collective-permute-start = (bf16[16,1024]{1,0:T(8,128)(2,1)S(1)}, bf16[16,1024]{1,0:T(8,128)(2,1)S(1)}, u32[]{:S(2)}, u32[]{:S(2)}) collective-permute-start(bf16[16,1024]{1,0:T(8,128)(2,1)S(1)} %bitcast.55), channel_id=1, source_target_pairs={{64,0},{128,64},{192,128},{256,192},{320,256},{384,320},{448,384},... | collective-permute-start | bytes 98312 | tf_op jit(solution)/shard_map/while/body/eval_jaxpr/ppermute | solution.py:15
  213.2 17.1 %all-to-all-start = ((bf16[64,2,1024]{2,1,0:T(2,128)(2,1)}), bf16[64,2,1024]{2,1,0:T(2,128)(2,1)S(1)}, u32[]{:S(2)}, u32[]{:S(2)}) async-start(bf16[64,2,1024]{2,1,0:T(2,128)(2,1)} %reshape.196), calls=%async_computation | async-start | bytes 524288 | tf_op jit(solution)/shard_map/while/body/eval_jaxpr/all_to_all | solution.py:66
  236.8 8.4 %collective-permute-start.1 = (bf16[16,1024]{1,0:T(8,128)(2,1)S(1)}, bf16[16,1024]{1,0:T(8,128)(2,1)S(1)}, u32[]{:S(2)}, u32[]{:S(2)}) collective-permute-start(bf16[16,1024]{1,0:T(8,128)(2,1)S(1)} %get-tuple-element.366), channel_id=1, source_target_pairs={{0,64},{64,128},{128,192},{192,256},{256,320},{320,384},{384,448},... | collective-permute-start | bytes 98312 | tf_op jit(solution)/shard_map/while/body/eval_jaxpr/ppermute | solution.py:15
  245.2 27.5 %collective-permute-start = (bf16[16,1024]{1,0:T(8,128)(2,1)S(1)}, bf16[16,1024]{1,0:T(8,128)(2,1)S(1)}, u32[]{:S(2)}, u32[]{:S(2)}) collective-permute-start(bf16[16,1024]{1,0:T(8,128)(2,1)S(1)} %bitcast.55), channel_id=1, source_target_pairs={{64,0},{128,64},{192,128},{256,192},{320,256},{384,320},{448,384},... | collective-permute-start | bytes 98312 | tf_op jit(solution)/shard_map/while/body/eval_jaxpr/ppermute | solution.py:15
  249.1 17.1 %all-to-all-start = ((bf16[64,2,1024]{2,1,0:T(2,128)(2,1)}), bf16[64,2,1024]{2,1,0:T(2,128)(2,1)S(1)}, u32[]{:S(2)}, u32[]{:S(2)}) async-start(bf16[64,2,1024]{2,1,0:T(2,128)(2,1)} %reshape.196), calls=%async_computation | async-start | bytes 524288 | tf_op jit(solution)/shard_map/while/body/eval_jaxpr/all_to_all | solution.py:66
  272.7 8.4 %collective-permute-start.1 = (bf16[16,1024]{1,0:T(8,128)(2,1)S(1)}, bf16[16,1024]{1,0:T(8,128)(2,1)S(1)}, u32[]{:S(2)}, u32[]{:S(2)}) collective-permute-start(bf16[16,1024]{1,0:T(8,128)(2,1)S(1)} %get-tuple-element.366), channel_id=1, source_target_pairs={{0,64},{64,128},{128,192},{192,256},{256,320},{320,384},{384,448},... | collective-permute-start | bytes 98312 | tf_op jit(solution)/shard_map/while/body/eval_jaxpr/ppermute | solution.py:15
  281.1 27.5 %collective-permute-start = (bf16[16,1024]{1,0:T(8,128)(2,1)S(1)}, bf16[16,1024]{1,0:T(8,128)(2,1)S(1)}, u32[]{:S(2)}, u32[]{:S(2)}) collective-permute-start(bf16[16,1024]{1,0:T(8,128)(2,1)S(1)} %bitcast.55), channel_id=1, source_target_pairs={{64,0},{128,64},{192,128},{256,192},{320,256},{384,320},{448,384},... | collective-permute-start | bytes 98312 | tf_op jit(solution)/shard_map/while/body/eval_jaxpr/ppermute | solution.py:15
  285.0 17.1 %all-to-all-start = ((bf16[64,2,1024]{2,1,0:T(2,128)(2,1)}), bf16[64,2,1024]{2,1,0:T(2,128)(2,1)S(1)}, u32[]{:S(2)}, u32[]{:S(2)}) async-start(bf16[64,2,1024]{2,1,0:T(2,128)(2,1)} %reshape.196), calls=%async_computation | async-start | bytes 524288 | tf_op jit(solution)/shard_map/while/body/eval_jaxpr/all_to_all | solution.py:66
  308.6 8.4 %collective-permute-start.1 = (bf16[16,1024]{1,0:T(8,128)(2,1)S(1)}, bf16[16,1024]{1,0:T(8,128)(2,1)S(1)}, u32[]{:S(2)}, u32[]{:S(2)}) collective-permute-start(bf16[16,1024]{1,0:T(8,128)(2,1)S(1)} %get-tuple-element.366), channel_id=1, source_target_pairs={{0,64},{64,128},{128,192},{192,256},{256,320},{320,384},{384,448},... | collective-permute-start | bytes 98312 | tf_op jit(solution)/shard_map/while/body/eval_jaxpr/ppermute | solution.py:15
  317.0 27.5 %collective-permute-start = (bf16[16,1024]{1,0:T(8,128)(2,1)S(1)}, bf16[16,1024]{1,0:T(8,128)(2,1)S(1)}, u32[]{:S(2)}, u32[]{:S(2)}) collective-permute-start(bf16[16,1024]{1,0:T(8,128)(2,1)S(1)} %bitcast.55), channel_id=1, source_target_pairs={{64,0},{128,64},{192,128},{256,192},{320,256},{384,320},{448,384},... | collective-permute-start | bytes 98312 | tf_op jit(solution)/shard_map/while/body/eval_jaxpr/ppermute | solution.py:15
  320.9 17.1 %all-to-all-start = ((bf16[64,2,1024]{2,1,0:T(2,128)(2,1)}), bf16[64,2,1024]{2,1,0:T(2,128)(2,1)S(1)}, u32[]{:S(2)}, u32[]{:S(2)}) async-start(bf16[64,2,1024]{2,1,0:T(2,128)(2,1)} %reshape.196), calls=%async_computation | async-start | bytes 524288 | tf_op jit(solution)/shard_map/while/body/eval_jaxpr/all_to_all | solution.py:66
  344.5 8.4 %collective-permute-start.1 = (bf16[16,1024]{1,0:T(8,128)(2,1)S(1)}, bf16[16,1024]{1,0:T(8,128)(2,1)S(1)}, u32[]{:S(2)}, u32[]{:S(2)}) collective-permute-start(bf16[16,1024]{1,0:T(8,128)(2,1)S(1)} %get-tuple-element.366), channel_id=1, source_target_pairs={{0,64},{64,128},{128,192},{192,256},{256,320},{320,384},{384,448},... | collective-permute-start | bytes 98312 | tf_op jit(solution)/shard_map/while/body/eval_jaxpr/ppermute | solution.py:15
  352.8 27.5 %collective-permute-start = (bf16[16,1024]{1,0:T(8,128)(2,1)S(1)}, bf16[16,1024]{1,0:T(8,128)(2,1)S(1)}, u32[]{:S(2)}, u32[]{:S(2)}) collective-permute-start(bf16[16,1024]{1,0:T(8,128)(2,1)S(1)} %bitcast.55), channel_id=1, source_target_pairs={{64,0},{128,64},{192,128},{256,192},{320,256},{384,320},{448,384},... | collective-permute-start | bytes 98312 | tf_op jit(solution)/shard_map/while/body/eval_jaxpr/ppermute | solution.py:15
  356.8 17.1 %all-to-all-start = ((bf16[64,2,1024]{2,1,0:T(2,128)(2,1)}), bf16[64,2,1024]{2,1,0:T(2,128)(2,1)S(1)}, u32[]{:S(2)}, u32[]{:S(2)}) async-start(bf16[64,2,1024]{2,1,0:T(2,128)(2,1)} %reshape.196), calls=%async_computation | async-start | bytes 524288 | tf_op jit(solution)/shard_map/while/body/eval_jaxpr/all_to_all | solution.py:66
  380.4 8.4 %collective-permute-start.1 = (bf16[16,1024]{1,0:T(8,128)(2,1)S(1)}, bf16[16,1024]{1,0:T(8,128)(2,1)S(1)}, u32[]{:S(2)}, u32[]{:S(2)}) collective-permute-start(bf16[16,1024]{1,0:T(8,128)(2,1)S(1)} %get-tuple-element.366), channel_id=1, source_target_pairs={{0,64},{64,128},{128,192},{192,256},{256,320},{320,384},{384,448},... | collective-permute-start | bytes 98312 | tf_op jit(solution)/shard_map/while/body/eval_jaxpr/ppermute | solution.py:15
  388.7 27.5 %collective-permute-start = (bf16[16,1024]{1,0:T(8,128)(2,1)S(1)}, bf16[16,1024]{1,0:T(8,128)(2,1)S(1)}, u32[]{:S(2)}, u32[]{:S(2)}) collective-permute-start(bf16[16,1024]{1,0:T(8,128)(2,1)S(1)} %bitcast.55), channel_id=1, source_target_pairs={{64,0},{128,64},{192,128},{256,192},{320,256},{384,320},{448,384},... | collective-permute-start | bytes 98312 | tf_op jit(solution)/shard_map/while/body/eval_jaxpr/ppermute | solution.py:15
  392.7 17.1 %all-to-all-start = ((bf16[64,2,1024]{2,1,0:T(2,128)(2,1)}), bf16[64,2,1024]{2,1,0:T(2,128)(2,1)S(1)}, u32[]{:S(2)}, u32[]{:S(2)}) async-start(bf16[64,2,1024]{2,1,0:T(2,128)(2,1)} %reshape.196), calls=%async_computation | async-start | bytes 524288 | tf_op jit(solution)/shard_map/while/body/eval_jaxpr/all_to_all | solution.py:66
  416.3 8.4 %collective-permute-start.1 = (bf16[16,1024]{1,0:T(8,128)(2,1)S(1)}, bf16[16,1024]{1,0:T(8,128)(2,1)S(1)}, u32[]{:S(2)}, u32[]{:S(2)}) collective-permute-start(bf16[16,1024]{1,0:T(8,128)(2,1)S(1)} %get-tuple-element.366), channel_id=1, source_target_pairs={{0,64},{64,128},{128,192},{192,256},{256,320},{320,384},{384,448},... | collective-permute-start | bytes 98312 | tf_op jit(solution)/shard_map/while/body/eval_jaxpr/ppermute | solution.py:15
  424.6 27.5 %collective-permute-start = (bf16[16,1024]{1,0:T(8,128)(2,1)S(1)}, bf16[16,1024]{1,0:T(8,128)(2,1)S(1)}, u32[]{:S(2)}, u32[]{:S(2)}) collective-permute-start(bf16[16,1024]{1,0:T(8,128)(2,1)S(1)} %bitcast.55), channel_id=1, source_target_pairs={{64,0},{128,64},{192,128},{256,192},{320,256},{384,320},{448,384},... | collective-permute-start | bytes 98312 | tf_op jit(solution)/shard_map/while/body/eval_jaxpr/ppermute | solution.py:15
  428.6 17.1 %all-to-all-start = ((bf16[64,2,1024]{2,1,0:T(2,128)(2,1)}), bf16[64,2,1024]{2,1,0:T(2,128)(2,1)S(1)}, u32[]{:S(2)}, u32[]{:S(2)}) async-start(bf16[64,2,1024]{2,1,0:T(2,128)(2,1)} %reshape.196), calls=%async_computation | async-start | bytes 524288 | tf_op jit(solution)/shard_map/while/body/eval_jaxpr/all_to_all | solution.py:66
  452.2 8.4 %collective-permute-start.1 = (bf16[16,1024]{1,0:T(8,128)(2,1)S(1)}, bf16[16,1024]{1,0:T(8,128)(2,1)S(1)}, u32[]{:S(2)}, u32[]{:S(2)}) collective-permute-start(bf16[16,1024]{1,0:T(8,128)(2,1)S(1)} %get-tuple-element.366), channel_id=1, source_target_pairs={{0,64},{64,128},{128,192},{192,256},{256,320},{320,384},{384,448},... | collective-permute-start | bytes 98312 | tf_op jit(solution)/shard_map/while/body/eval_jaxpr/ppermute | solution.py:15
  460.5 27.5 %collective-permute-start = (bf16[16,1024]{1,0:T(8,128)(2,1)S(1)}, bf16[16,1024]{1,0:T(8,128)(2,1)S(1)}, u32[]{:S(2)}, u32[]{:S(2)}) collective-permute-start(bf16[16,1024]{1,0:T(8,128)(2,1)S(1)} %bitcast.55), channel_id=1, source_target_pairs={{64,0},{128,64},{192,128},{256,192},{320,256},{384,320},{448,384},... | collective-permute-start | bytes 98312 | tf_op jit(solution)/shard_map/while/body/eval_jaxpr/ppermute | solution.py:15
  464.4 17.1 %all-to-all-start = ((bf16[64,2,1024]{2,1,0:T(2,128)(2,1)}), bf16[64,2,1024]{2,1,0:T(2,128)(2,1)S(1)}, u32[]{:S(2)}, u32[]{:S(2)}) async-start(bf16[64,2,1024]{2,1,0:T(2,128)(2,1)} %reshape.196), calls=%async_computation | async-start | bytes 524288 | tf_op jit(solution)/shard_map/while/body/eval_jaxpr/all_to_all | solution.py:66
  488.0 8.4 %collective-permute-start.1 = (bf16[16,1024]{1,0:T(8,128)(2,1)S(1)}, bf16[16,1024]{1,0:T(8,128)(2,1)S(1)}, u32[]{:S(2)}, u32[]{:S(2)}) collective-permute-start(bf16[16,1024]{1,0:T(8,128)(2,1)S(1)} %get-tuple-element.366), channel_id=1, source_target_pairs={{0,64},{64,128},{128,192},{192,256},{256,320},{320,384},{384,448},... | collective-permute-start | bytes 98312 | tf_op jit(solution)/shard_map/while/body/eval_jaxpr/ppermute | solution.py:15
  496.4 27.5 %collective-permute-start = (bf16[16,1024]{1,0:T(8,128)(2,1)S(1)}, bf16[16,1024]{1,0:T(8,128)(2,1)S(1)}, u32[]{:S(2)}, u32[]{:S(2)}) collective-permute-start(bf16[16,1024]{1,0:T(8,128)(2,1)S(1)} %bitcast.55), channel_id=1, source_target_pairs={{64,0},{128,64},{192,128},{256,192},{320,256},{384,320},{448,384},... | collective-permute-start | bytes 98312 | tf_op jit(solution)/shard_map/while/body/eval_jaxpr/ppermute | solution.py:15
  500.3 17.1 %all-to-all-start = ((bf16[64,2,1024]{2,1,0:T(2,128)(2,1)}), bf16[64,2,1024]{2,1,0:T(2,128)(2,1)S(1)}, u32[]{:S(2)}, u32[]{:S(2)}) async-start(bf16[64,2,1024]{2,1,0:T(2,128)(2,1)} %reshape.196), calls=%async_computation | async-start | bytes 524288 | tf_op jit(solution)/shard_map/while/body/eval_jaxpr/all_to_all | solution.py:66
  523.9 8.4 %collective-permute-start.1 = (bf16[16,1024]{1,0:T(8,128)(2,1)S(1)}, bf16[16,1024]{1,0:T(8,128)(2,1)S(1)}, u32[]{:S(2)}, u32[]{:S(2)}) collective-permute-start(bf16[16,1024]{1,0:T(8,128)(2,1)S(1)} %get-tuple-element.366), channel_id=1, source_target_pairs={{0,64},{64,128},{128,192},{192,256},{256,320},{320,384},{384,448},... | collective-permute-start | bytes 98312 | tf_op jit(solution)/shard_map/while/body/eval_jaxpr/ppermute | solution.py:15
  532.3 27.5 %collective-permute-start = (bf16[16,1024]{1,0:T(8,128)(2,1)S(1)}, bf16[16,1024]{1,0:T(8,128)(2,1)S(1)}, u32[]{:S(2)}, u32[]{:S(2)}) collective-permute-start(bf16[16,1024]{1,0:T(8,128)(2,1)S(1)} %bitcast.55), channel_id=1, source_target_pairs={{64,0},{128,64},{192,128},{256,192},{320,256},{384,320},{448,384},... | collective-permute-start | bytes 98312 | tf_op jit(solution)/shard_map/while/body/eval_jaxpr/ppermute | solution.py:15
  536.2 17.1 %all-to-all-start = ((bf16[64,2,1024]{2,1,0:T(2,128)(2,1)}), bf16[64,2,1024]{2,1,0:T(2,128)(2,1)S(1)}, u32[]{:S(2)}, u32[]{:S(2)}) async-start(bf16[64,2,1024]{2,1,0:T(2,128)(2,1)} %reshape.196), calls=%async_computation | async-start | bytes 524288 | tf_op jit(solution)/shard_map/while/body/eval_jaxpr/all_to_all | solution.py:66
  559.8 8.4 %collective-permute-start.1 = (bf16[16,1024]{1,0:T(8,128)(2,1)S(1)}, bf16[16,1024]{1,0:T(8,128)(2,1)S(1)}, u32[]{:S(2)}, u32[]{:S(2)}) collective-permute-start(bf16[16,1024]{1,0:T(8,128)(2,1)S(1)} %get-tuple-element.366), channel_id=1, source_target_pairs={{0,64},{64,128},{128,192},{192,256},{256,320},{320,384},{384,448},... | collective-permute-start | bytes 98312 | tf_op jit(solution)/shard_map/while/body/eval_jaxpr/ppermute | solution.py:15
  568.2 0.6 copy-start
where the time goes:
time: 571 us; the launch traced here: 569 us
  starting transfers between devices  218 us (38%)
  waiting for transfers between devices  204 us (36%)
  matrix products  82.5 us (14%)
  local copies, waits for them, and re-layouts  56.7 us (10%)
  other arithmetic  6.01 us (1%)
    all_to_all x15, waiting for transfers between devices, layer(): lax.all_to_all(outgoing, 'neuron', split_axis=0, concat_axis=0, tiled=True)  189 us
    ppermute x30, starting transfers between devices, passed_along(): lax.ppermute(value, axis, [(source, source + steps) for source in range(f...  142 us
    all_to_all x15, starting transfers between devices, layer(): lax.all_to_all(outgoing, 'neuron', split_axis=0, concat_axis=0, tiled=True)  75.6 us
    dot_general x15, matrix products, layer(): jnp.einsum('kri,kio->kro', inputs, weights, preferred_element_type=jnp.fl...  51.8 us
    dot_general x15, matrix products, layer(): jnp.einsum('kc,kro->rco', col_onehot, partial_value, precision=lax.Precis...  25.9 us
    while x30, local copies, waits for them, and re-layouts  19.9 us
    ppermute x30, waiting for transfers between devices, passed_along(): lax.ppermute(value, axis, [(source, source + steps) for source in range(f...  15 us
    gather x15, local copies, waits for them, and re-layouts, layer(): inputs = jnp.take(incoming, slot_of_tile, axis=0)  12.7 us
  transfers between devices with their start and end apart: 45, of which 30 were waited for; matrix products, arithmetic and copies ran while one was open for 22% of the time, Pallas kernels for 0%

commit v1 on v0

v1 whole, which is shorter than its diff:
```python
import functools

import jax
import jax.numpy as jnp
from jax import lax
from jax.experimental import pallas as pl
from jax.experimental.pallas import tpu as pltpu
from jax.sharding import PartitionSpec as P

BS = 64
CLAMP_TOP = 32.0
LANES = 128
GROUP = 8
INDEX_ROWS = 5


def reorder_kernel(in_ref, out_ref):
    groups = out_ref.shape[0]
    half = in_ref.shape[1]
    low = lax.broadcasted_iota(jnp.int32, (half, LANES), 1) < BS
    for group in range(groups):
        for pair in range(GROUP // 2):
            first = in_ref[group * GROUP + 2 * pair].astype(jnp.float32)
            second = in_ref[group * GROUP + 2 * pair + 1].astype(jnp.float32)
            even = jnp.where(low, first, pltpu.roll(second, BS, 1))
            odd = jnp.where(low, pltpu.roll(first, BS, 1), second)
            at = pair * 2 * half
            out_ref[group, at : at + half, :] = even.astype(out_ref.dtype)
            out_ref[group, at + half : at + 2 * half, :] = odd.astype(out_ref.dtype)


def reorder_tiles(slabs):
    tiles, half, _ = slabs.shape
    steps = 4
    per_step = tiles // steps
    return pl.pallas_call(
        reorder_kernel,
        grid=(steps,),
        in_specs=[pl.BlockSpec((per_step, half, LANES), lambda i: (i, 0, 0))],
        out_specs=pl.BlockSpec((per_step // GROUP, GROUP * half, LANES), lambda i: (i, 0, 0)),
        out_shape=jax.ShapeDtypeStruct((tiles // GROUP, GROUP * half, LANES), slabs.dtype),
        name="reorder_tiles",
    )(slabs)


def parity_position(lane):
    within = lane % BS
    return 2 * (within % (BS // 2)) + within // (BS // 2)


def spread_matrix(offset):
    row = lax.broadcasted_iota(jnp.int32, (LANES, 2 * LANES), 0)
    col = lax.broadcasted_iota(jnp.int32, (LANES, 2 * LANES), 1)
    lane = col % LANES
    wanted_half = (col // LANES) == (lane // BS)
    hit = wanted_half & (row == parity_position(lane) + offset)
    return hit.astype(jnp.float32).astype(jnp.bfloat16)


def pack_blocks(index_ref, pick_at, low_ref, high_ref, out_ref):
    shards = out_ref.shape[0]
    for shard in range(shards):
        first = index_ref[pick_at + shard]
        second = index_ref[pick_at + shards + shard]
        out_ref[shard] = low_ref[first] + high_ref[second]


def first_pack_kernel(pick_at, index_ref, in_ref, out_ref, low_ref, high_ref):
    rows, width = in_ref.shape
    for offset in range(2):
        spread = spread_matrix(offset * BS)
        for tile in range(width // LANES):
            value = jnp.dot(
                in_ref[:, tile * LANES : (tile + 1) * LANES], spread, preferred_element_type=jnp.float32
            ).astype(jnp.bfloat16)
            low_ref[2 * tile + offset] = value[:, :LANES]
            high_ref[2 * tile + offset] = value[:, LANES:]
    pack_blocks(index_ref, pick_at, low_ref, high_ref, out_ref)


def first_pack(index, features, shards, pick_at):
    rows, width = features.shape
    blocks = width // BS
    return pl.pallas_call(
        functools.partial(first_pack_kernel, pick_at),
        grid_spec=pltpu.PrefetchScalarGridSpec(
            num_scalar_prefetch=1,
            grid=(1,),
            in_specs=[pl.BlockSpec((rows, width), lambda i, index: (0, 0))],
            out_specs=pl.BlockSpec((shards, rows, LANES), lambda i, index: (0, 0, 0)),
            scratch_shapes=[pltpu.VMEM((blocks, rows, LANES), jnp.bfloat16)] * 2,
        ),
        out_shape=jax.ShapeDtypeStruct((shards, rows, LANES), jnp.bfloat16),
        name="first_pack",
    )(index, features)


def layer_kernel(index_at, pick_at, index_ref, in_ref, tiles_ref, bias_ref, out_ref, spread_ref, total_ref, low_ref, high_ref):
    step = pl.program_id(0)
    steps = pl.num_programs(0)
    shards, rows, _ = in_ref.shape
    groups = tiles_ref.shape[0]
    tile_slots = groups * GROUP * steps
    blocks = total_ref.shape[1] - 1

    @pl.when(step == 0)
    def _():
        total_ref[...] = jnp.zeros_like(total_ref)
        low = lax.broadcasted_iota(jnp.int32, (rows, LANES), 1) < BS
        for shard in range(shards):
            value = in_ref[shard].astype(jnp.float32)
            turned = pltpu.roll(value, BS, 1)
            spread_ref[0, 2 * shard] = jnp.where(low, value, 0.0).astype(jnp.bfloat16)
            spread_ref[0, 2 * shard + 1] = jnp.where(low, turned, 0.0).astype(jnp.bfloat16)
            spread_ref[1, 2 * shard] = jnp.where(low, 0.0, turned).astype(jnp.bfloat16)
            spread_ref[1, 2 * shard + 1] = jnp.where(low, 0.0, value).astype(jnp.bfloat16)

    empty = jnp.zeros((rows, LANES), jnp.bfloat16)
    for group in range(groups):
        first_tile = (step * groups + group) * GROUP
        left = []
        right = []
        for member in range(GROUP):
            pair = member // 2
            slot = index_ref[index_at + first_tile + member]
            value = spread_ref[pair % 2, slot]
            left.append(value if pair < 2 else empty)
            right.append(value if pair >= 2 else empty)
        gathered = jnp.concatenate([jnp.concatenate(left, axis=0), jnp.concatenate(right, axis=0)], axis=1)
        product = jnp.dot(gathered, tiles_ref[group], preferred_element_type=jnp.float32)
        for member in range(GROUP):
            column = index_ref[index_at + tile_slots + first_tile + member]
            total_ref[member % 2, column] += product[member * rows : (member + 1) * rows]

    @pl.when(step == steps - 1)
    def _():
        even = total_ref[0, :blocks].reshape(blocks * rows, LANES)
        odd = total_ref[1, :blocks].reshape(blocks * rows, LANES)
        summed = (even + pltpu.roll(odd, BS, 1)).reshape(blocks, rows, LANES) + bias_ref[...][:, None, :]
        result = jnp.clip(summed, 0.0, CLAMP_TOP)
        if pick_at is None:
            low = lax.broadcasted_iota(jnp.int32, (rows, LANES), 1) < BS
            for tile in range(blocks // 2):
                value = jnp.where(low, result[2 * tile], pltpu.roll(result[2 * tile + 1], BS, 1))
                out_ref[:, tile * LANES : (tile + 1) * LANES] = value.astype(out_ref.dtype)
        else:
            value = jnp.dot(
                result.astype(jnp.bfloat16).reshape(blocks * rows, LANES),
                spread_matrix(0),
                preferred_element_type=jnp.float32,
            ).astype(jnp.bfloat16)
            low_ref[...] = value[:, :LANES].reshape(blocks, rows, LANES)
            high_ref[...] = value[:, LANES:].reshape(blocks, rows, LANES)
            pack_blocks(index_ref, pick_at, low_ref, high_ref, out_ref)


def run_layer(index, incoming, weights, bias, layer, blocks, last):
    shards, rows, _ = incoming.shape
    groups, depth = weights.shape[1:3]
    tile_slots = groups * GROUP
    steps = 4
    stride = INDEX_ROWS * LANES
    pick_at = None if last else (layer + 1) * stride + 2 * tile_slots
    if last:
        out_shape = (rows, blocks * BS)
    else:
        out_shape = (shards, rows, LANES)
    zeros = (0,) * len(out_shape)
    return pl.pallas_call(
        functools.partial(layer_kernel, layer * stride, pick_at),
        grid_spec=pltpu.PrefetchScalarGridSpec(
            num_scalar_prefetch=1,
            grid=(steps,),
            in_specs=[
                pl.BlockSpec((shards, rows, LANES), lambda i, index: (0, 0, 0)),
                pl.BlockSpec((None, groups // steps, depth, LANES), lambda i, index: (layer, i, 0, 0)),
                pl.BlockSpec((None, blocks, LANES), lambda i, index: (layer, 0, 0)),
            ],
            out_specs=pl.BlockSpec(out_shape, lambda i, index: zeros),
            scratch_shapes=[
                pltpu.VMEM((2, 2 * shards, rows, LANES), jnp.bfloat16),
                pltpu.VMEM((2, blocks + 1, rows, LANES), jnp.float32),
                pltpu.VMEM((blocks, rows, LANES), jnp.bfloat16),
                pltpu.VMEM((blocks, rows, LANES), jnp.bfloat16),
            ],
        ),
        out_shape=jax.ShapeDtypeStruct(out_shape, jnp.bfloat16),
        name="layer_step",
    )(index, incoming, weights, bias)


def plan_routes(tile_row, tile_col, tile_count, own_index, blocks_dev):
    shards = tile_count.shape[0]
    tile_slots = tile_col.shape[0]
    slot_ids = jnp.arange(tile_slots, dtype=jnp.int32)
    rows = tile_row.reshape(shards, tile_slots)
    own_rows = lax.dynamic_index_in_dim(rows, own_index, 0, keepdims=False)
    own_used = slot_ids < tile_count[own_index]
    own_shards = own_rows // blocks_dev
    earlier = (own_shards[None, :] == own_shards[:, None]) & (own_rows[None, :] < own_rows[:, None]) & own_used[None, :]
    rank = jnp.any(earlier, axis=1).astype(jnp.int32)
    slot = jnp.where(own_used, 2 * own_shards + rank, 0)
    column = jnp.where(own_used, tile_col, blocks_dev)
    wanted = (rows // blocks_dev == own_index) & (slot_ids[None, :] < tile_count[:, None])
    local = rows - own_index * blocks_dev
    lowest = jnp.min(jnp.where(wanted, local, blocks_dev - 1), axis=1)
    highest = jnp.max(jnp.where(wanted, local, 0), axis=1)
    return jnp.concatenate([slot, column, lowest, highest])


def body(features, tiles, tile_row, tile_col, tile_count, bias):
    shards = lax.axis_size("neuron")
    layers = lax.axis_size("section")
    own_index = lax.axis_index("neuron")
    rows, width = features.shape
    blocks = width // BS
    tile_slots = tiles.shape[1]
    with jax.named_scope("tile_order"):
        slabs = tiles[0].reshape(tile_slots, BS * BS // LANES, LANES)
        ordered = reorder_tiles(slabs)
    with jax.named_scope("weight_gather"):
        weights = lax.all_gather(ordered, "section", axis=0)
    with jax.named_scope("routes"):
        routes = plan_routes(tile_row[0], tile_col[0], tile_count[0], own_index, blocks)
        own = jnp.concatenate(
            [
                routes.astype(jnp.float32).reshape(INDEX_ROWS, LANES),
                jnp.zeros((8 - INDEX_ROWS, LANES), jnp.float32),
                bias[0].reshape(width // LANES, LANES),
            ]
        )
        shared = lax.all_to_all(jnp.broadcast_to(own[None], (layers,) + own.shape), "section", 0, 0, tiled=True)
        index = shared[:, :INDEX_ROWS].astype(jnp.int32).reshape(-1)
        biases = shared[:, 8:].reshape(layers, blocks, BS)
        biases = jnp.pad(biases, ((0, 0), (0, 0), (0, LANES - BS)))
    with jax.named_scope("layers"):
        outgoing = first_pack(index, features, shards, 2 * tile_slots)
        for layer in range(layers):
            incoming = lax.all_to_all(outgoing, "neuron", 0, 0, tiled=True)
            outgoing = run_layer(index, incoming, weights, biases, layer, blocks, layer == layers - 1)
    return outgoing


def solution(mesh):
    in_specs = (
        P("section", "neuron"),
        P("section", "neuron", None),
        P("section", None),
        P("section", "neuron"),
        P("section", None),
        P("section", "neuron"),
    )
    out_specs = P("section", "neuron")
    return jax.shard_map(body, mesh=mesh, in_specs=in_specs, out_specs=out_specs, check_vma=False)
```

time: 571 us -> 306 us (0.54)
  the two profiles are of different devices: /device:TPU:1 before, /device:TPU:2 now
where the time goes in v1:
time: 306 us; the launch traced here: 304 us
  blocking collectives  155 us (51%)
  waiting for transfers between devices  60.9 us (20%)
  Pallas kernels  53 us (17%)
  between operations  13.5 us (4%)
  starting transfers between devices  12.9 us (4%)
  local copies, waits for them, and re-layouts  6.24 us (2%)
    all_to_all x7, blocking collectives, body(): incoming = lax.all_to_all(outgoing, 'neuron', 0, 0, tiled=True)  142 us
    all_gather x1, waiting for transfers between devices, body(): weights = lax.all_gather(ordered, 'section', axis=0)  46.8 us
    pallas_call x8, Pallas kernels, run_layer(): pl.pallas_call(functools.partial(layer_kernel, layer * stride, pick_at),...  46 us
    all_to_all x1, waiting for transfers between devices, body(): incoming = lax.all_to_all(outgoing, 'neuron', 0, 0, tiled=True)  14.1 us
    all_to_all x1, starting transfers between devices, body(): incoming = lax.all_to_all(outgoing, 'neuron', 0, 0, tiled=True)  12.9 us
    all_to_all x1, blocking collectives, body(): lax.all_to_all(jnp.broadcast_to(own[None], (layers,) + own.shape), 'secti...  12.4 us
  transfers between devices with their start and end apart: 2, of which 2 were waited for; matrix products, arithmetic and copies ran while one was open for 2% of the time, Pallas kernels for 1%

profile of v1, /device:TPU:2, one launch (start us, length us, event | category | flops | bytes accessed | tf_op | source)
XLA Modules:
  0.0 304.2 jit_solution(14474918847553871202)
XLA Ops:
  6.5 0.0 all-gather.3.cloned.1.call-start
  6.5 3.4 %copy.7 = bf16[32,8,32,128]{3,2,1,0:T(8,128)(2,1)} copy(bf16[32,8,32,128]{3,1,2,0:T(8,128)(2,1)} %bitcast.21) | data formatting | bytes 4194304
  10.0 4.2 %reorder_tiles.1 = bf16[32,256,128]{2,1,0:T(8,128)(2,1)} custom-call(bf16[256,32,128]{2,1,0:T(8,128)(2,1)} %bitcast.20), custom_call_target="tpu_custom_call" | custom-call | tf_op jit(solution)/shard_map/tile_order/reorder_tiles/pallas_call | solution.py:36
  14.1 0.0 copy-start.1
  14.1 0.0 copy-start.4
  14.1 0.0 copy-start.3
  14.1 0.0 copy-start.2
  14.1 0.0 all-gather.3.cloned.1.call-update
  14.2 0.5 broadcast.184
  14.7 0.3 copy-done.1
  15.0 0.8 reduce.3
  15.8 0.0 copy-done.4
  15.8 0.6 constant_dynamic-slice_fusion.1
  16.4 0.1 pad.6.clone
  16.5 0.6 iota_compare_fusion.1
  17.2 0.2 and_reduce_fusion
  17.4 0.2 select_reduce_fusion.1
  17.6 0.0 copy-done.3
  17.6 0.7 add_select_fusion.1
  18.3 0.1 fusion.4
  18.3 0.0 copy-done.2
  18.3 0.1 pad_maximum_fusion
  18.4 12.4 %all_to_all.45 = f32[8,16,128]{2,1,0:T(8,128)S(1)} all-to-all(f32[8,16,128]{2,1,0:T(8,128)S(1)} %broadcast_in_dim.11), channel_id=1, replica_groups=mesh['section'=8,'neuron'=64] {'section'}, dimensions={0} | all-to-all | bytes 131072 | tf_op jit(solution)/shard_map/routes/all_to_all | solution.py:232
  30.9 0.6 reshape.63.index_ref
  31.5 2.8 first_pack.1
  34.3 12.9 %all-to-all-start.1 = ((bf16[64,16,128]{2,1,0:T(8,128)(2,1)}), bf16[64,16,128]{2,1,0:T(8,128)(2,1)S(1)}, u32[]{:S(2)}, u32[]{:S(2)}) async-start(bf16[64,16,128]{2,1,0:T(8,128)(2,1)} %first_pack.1), calls=%async_computation.1 | async-start | bytes 524288 | tf_op jit(solution)/shard_map/layers/all_to_all | solution.py:239
  47.2 0.1 reshape.64
  47.3 0.6 pad.4.bias_ref
  48.0 14.1 %all-to-all-done.1.in_ref = bf16[64,16,128]{2,1,0:T(8,128)(2,1)S(1)} async-done(((bf16[64,16,128]{2,1,0:T(8,128)(2,1)}), bf16[64,16,128]{2,1,0:T(8,128)(2,1)S(1)}, u32[]{:S(2)}, u32[]{:S(2)}) %all-to-all-start.1) | async-done | bytes 262176 | tf_op jit(solution)/shard_map/layers/all_to_all | solution.py:239
  62.1 0.0 copy-start
  62.1 46.8 %all-gather.3.cloned.1.call-done = bf16[256,256,128]{2,1,0:T(8,128)(2,1)} async-done(((bf16[32,256,128]{2,1,0:T(8,128)(2,1)}), bf16[256,256,128]{2,1,0:T(8,128)(2,1)}) %all-gather.3.cloned.1.call-update) | async-done | bytes 16777232 | tf_op jit(solution)/shard_map/weight_gather/all_gather | solution.py:222
  108.9 0.0 copy-done
  108.9 5.8 %layer_step.8 = bf16[64,16,128]{2,1,0:T(8,128)(2,1)} custom-call(s32[5120]{0:T(1024)} %reshape.63.index_ref, bf16[64,16,128]{2,1,0:T(8,128)(2,1)} %copy-done, bf16[8,32,256,128]{3,2,1,0:T(8,128)(2,1)} %bitcast.12, f32[8,16,128]{2,1,0:T(8,128)} %pad.4.bias_ref), custom_call_target="tpu_custom_call" | custom-call | tf_op jit(solution)/shard_map/layers/layer_step/pallas_call | solution.py:169
  114.7 28.7 %all_to_all.46.in_ref = bf16[64,16,128]{2,1,0:T(8,128)(2,1)} all-to-all(bf16[64,16,128]{2,1,0:T(8,128)(2,1)} %layer_step.8), channel_id=1, replica_groups=mesh['section'=8,'neuron'=64] {'neuron'}, dimensions={0} | all-to-all | bytes 524288 | tf_op jit(solution)/shard_map/layers/all_to_all | solution.py:239
  143.4 5.8 %layer_step.9 = bf16[64,16,128]{2,1,0:T(8,128)(2,1)} custom-call(s32[5120]{0:T(1024)} %reshape.63.index_ref, bf16[64,16,128]{2,1,0:T(8,128)(2,1)} %all_to_all.46.in_ref, bf16[8,32,256,128]{3,2,1,0:T(8,128)(2,1)} %bitcast.13, f32[8,16,128]{2,1,0:T(8,128)} %pad.4.bias_ref), custom_call_target="tpu_custom_call" | custom-call | tf_op jit(solution)/shard_map/layers/layer_step/pallas_call | solution.py:169
  149.2 19.0 %all_to_all.47.in_ref = bf16[64,16,128]{2,1,0:T(8,128)(2,1)} all-to-all(bf16[64,16,128]{2,1,0:T(8,128)(2,1)} %layer_step.9), channel_id=1, replica_groups=mesh['section'=8,'neuron'=64] {'neuron'}, dimensions={0} | all-to-all | bytes 524288 | tf_op jit(solution)/shard_map/layers/all_to_all | solution.py:239
  168.2 5.8 %layer_step.10 = bf16[64,16,128]{2,1,0:T(8,128)(2,1)} custom-call(s32[5120]{0:T(1024)} %reshape.63.index_ref, bf16[64,16,128]{2,1,0:T(8,128)(2,1)} %all_to_all.47.in_ref, bf16[8,32,256,128]{3,2,1,0:T(8,128)(2,1)} %bitcast.14, f32[8,16,128]{2,1,0:T(8,128)} %pad.4.bias_ref), custom_call_target="tpu_custom_call" | custom-call | tf_op jit(solution)/shard_map/layers/layer_step/pallas_call | solution.py:169
  174.0 18.9 %all_to_all.48.in_ref = bf16[64,16,128]{2,1,0:T(8,128)(2,1)} all-to-all(bf16[64,16,128]{2,1,0:T(8,128)(2,1)} %layer_step.10), channel_id=1, replica_groups=mesh['section'=8,'neuron'=64] {'neuron'}, dimensions={0} | all-to-all | bytes 524288 | tf_op jit(solution)/shard_map/layers/all_to_all | solution.py:239
  193.0 5.8 %layer_step.11 = bf16[64,16,128]{2,1,0:T(8,128)(2,1)} custom-call(s32[5120]{0:T(1024)} %reshape.63.index_ref, bf16[64,16,128]{2,1,0:T(8,128)(2,1)} %all_to_all.48.in_ref, bf16[8,32,256,128]{3,2,1,0:T(8,128)(2,1)} %bitcast.15, f32[8,16,128]{2,1,0:T(8,128)} %pad.4.bias_ref), custom_call_target="tpu_custom_call" | custom-call | tf_op jit(solution)/shard_map/layers/layer_step/pallas_call | solution.py:169
  198.8 18.9 %all_to_all.49.in_ref = bf16[64,16,128]{2,1,0:T(8,128)(2,1)} all-to-all(bf16[64,16,128]{2,1,0:T(8,128)(2,1)} %layer_step.11), channel_id=1, replica_groups=mesh['section'=8,'neuron'=64] {'neuron'}, dimensions={0} | all-to-all | bytes 524288 | tf_op jit(solution)/shard_map/layers/all_to_all | solution.py:239
  217.7 5.8 %layer_step.12 = bf16[64,16,128]{2,1,0:T(8,128)(2,1)} custom-call(s32[5120]{0:T(1024)} %reshape.63.index_ref, bf16[64,16,128]{2,1,0:T(8,128)(2,1)} %all_to_all.49.in_ref, bf16[8,32,256,128]{3,2,1,0:T(8,128)(2,1)} %bitcast.16, f32[8,16,128]{2,1,0:T(8,128)} %pad.4.bias_ref), custom_call_target="tpu_custom_call" | custom-call | tf_op jit(solution)/shard_map/layers/layer_step/pallas_call | solution.py:169
  223.5 18.9 %all_to_all.50.in_ref = bf16[64,16,128]{2,1,0:T(8,128)(2,1)} all-to-all(bf16[64,16,128]{2,1,0:T(8,128)(2,1)} %layer_step.12), channel_id=1, replica_groups=mesh['section'=8,'neuron'=64] {'neuron'}, dimensions={0} | all-to-all | bytes 524288 | tf_op jit(solution)/shard_map/layers/all_to_all | solution.py:239
  242.4 5.8 %layer_step.13 = bf16[64,16,128]{2,1,0:T(8,128)(2,1)} custom-call(s32[5120]{0:T(1024)} %reshape.63.index_ref, bf16[64,16,128]{2,1,0:T(8,128)(2,1)} %all_to_all.50.in_ref, bf16[8,32,256,128]{3,2,1,0:T(8,128)(2,1)} %bitcast.17, f32[8,16,128]{2,1,0:T(8,128)} %pad.4.bias_ref), custom_call_target="tpu_custom_call" | custom-call | tf_op jit(solution)/shard_map/layers/layer_step/pallas_call | solution.py:169
  248.2 18.9 %all_to_all.51.in_ref = bf16[64,16,128]{2,1,0:T(8,128)(2,1)} all-to-all(bf16[64,16,128]{2,1,0:T(8,128)(2,1)} %layer_step.13), channel_id=1, replica_groups=mesh['section'=8,'neuron'=64] {'neuron'}, dimensions={0} | all-to-all | bytes 524288 | tf_op jit(solution)/shard_map/layers/all_to_all | solution.py:239
  267.2 5.8 %layer_step.14 = bf16[64,16,128]{2,1,0:T(8,128)(2,1)} custom-call(s32[5120]{0:T(1024)} %reshape.63.index_ref, bf16[64,16,128]{2,1,0:T(8,128)(2,1)} %all_to_all.51.in_ref, bf16[8,32,256,128]{3,2,1,0:T(8,128)(2,1)} %bitcast.18, f32[8,16,128]{2,1,0:T(8,128)} %pad.4.bias_ref), custom_call_target="tpu_custom_call" | custom-call | tf_op jit(solution)/shard_map/layers/layer_step/pallas_call | solution.py:169
  272.9 19.0 %all_to_all.52.in_ref = bf16[64,16,128]{2,1,0:T(8,128)(2,1)} all-to-all(bf16[64,16,128]{2,1,0:T(8,128)(2,1)} %layer_step.14), channel_id=1, replica_groups=mesh['section'=8,'neuron'=64] {'neuron'}, dimensions={0} | all-to-all | bytes 524288 | tf_op jit(solution)/shard_map/layers/all_to_all | solution.py:239
  291.9 5.5 %layer_step.15 = bf16[16,1024]{1,0:T(8,128)(2,1)} custom-call(s32[5120]{0:T(1024)} %reshape.63.index_ref, bf16[64,16,128]{2,1,0:T(8,128)(2,1)} %all_to_all.52.in_ref, bf16[8,32,256,128]{3,2,1,0:T(8,128)(2,1)} %bitcast.19, f32[8,16,128]{2,1,0:T(8,128)} %pad.4.bias_ref), custom_call_target="tpu_custom_call" | custom-call | tf_op jit(solution)/shard_map/layers/layer_step/pallas_call | solution.py:169
  (7 shorter events, 0.1 us)
Async XLA Ops:
  6.5 102.3 %all-gather.3.cloned.1.call-start = ((), (), s32[]{:S(2)}) async-start(), calls=%async_computation.9 | async-start | bytes 18874368 | tf_op jit(solution)/shard_map/weight_gather/all_gather | solution.py:222
  14.1 0.8 copy-start.1
  14.1 1.7 copy-start.4
  14.1 3.5 %copy-start.3 = (s32[1,256]{1,0:T(1,128)S(1)}, s32[1,256]{1,0:T(1,128)}, u32[]{:S(2)}) copy-start(s32[1,256]{1,0:T(1,128)} %param.9) | copy-start | bytes 3076
  14.1 4.2 %copy-start.2 = (f32[1,1024]{1,0:T(1,128)S(1)}, f32[1,1024]{1,0:T(1,128)}, u32[]{:S(2)}) copy-start(f32[1,1024]{1,0:T(1,128)} %param.11) | copy-start | bytes 12292
  34.3 27.8 %all-to-all-start.1 = ((bf16[64,16,128]{2,1,0:T(8,128)(2,1)}), bf16[64,16,128]{2,1,0:T(8,128)(2,1)S(1)}, u32[]{:S(2)}, u32[]{:S(2)}) async-start(bf16[64,16,128]{2,1,0:T(8,128)(2,1)} %first_pack.1), calls=%async_computation.1 | async-start | bytes 524288 | tf_op jit(solution)/shard_map/layers/all_to_all | solution.py:239
  62.1 46.8 %copy-start = (bf16[64,16,128]{2,1,0:T(8,128)(2,1)}, bf16[64,16,128]{2,1,0:T(8,128)(2,1)S(1)}, u32[]{:S(2)}) copy-start(bf16[64,16,128]{2,1,0:T(8,128)(2,1)S(1)} %all-to-all-done.1.in_ref) | copy-start | bytes 786436
Sparse Core Ops, SparseCore 0:
  14.3 94.5 all-gather.2

commit v2 on v1

v2 whole, which is shorter than its diff:
```python
import functools

import jax
import jax.numpy as jnp
from jax import lax
from jax.experimental import pallas as pl
from jax.experimental.pallas import tpu as pltpu
from jax.sharding import PartitionSpec as P

BS = 64
CLAMP_TOP = 32.0
LANES = 128
GROUP = 8
INDEX_STRIDE = 1024
PICKS_AT = 512
VMEM_LIMIT = 48 << 20


def reorder_kernel(in_ref, out_ref, move_ref):
    groups, depth, _ = in_ref.shape
    half = depth // GROUP
    pairs = GROUP // 2

    @pl.when(pl.program_id(0) == 0)
    def _():
        row = lax.broadcasted_iota(jnp.int32, (depth, depth), 0)
        col = lax.broadcasted_iota(jnp.int32, (depth, depth), 1)
        parity = row // (pairs * half)
        pair = row // half % pairs
        slab = row % half
        hit = col == slab * GROUP + 2 * pair + parity
        move_ref[...] = hit.astype(jnp.float32).astype(jnp.bfloat16)

    low = lax.broadcasted_iota(jnp.int32, (half, LANES), 1) < BS
    for group in range(groups):
        moved = jnp.dot(move_ref[...], in_ref[group], preferred_element_type=jnp.float32)
        for pair in range(pairs):
            first = moved[pair * half : (pair + 1) * half]
            second = moved[(pairs + pair) * half : (pairs + pair + 1) * half]
            even = jnp.where(low, first, pltpu.roll(second, BS, 1))
            odd = jnp.where(low, pltpu.roll(first, BS, 1), second)
            at = pair * 2 * half
            out_ref[group, at : at + half, :] = even.astype(out_ref.dtype)
            out_ref[group, at + half : at + 2 * half, :] = odd.astype(out_ref.dtype)


def reorder_tiles(bands):
    groups, depth, _ = bands.shape
    steps = 4
    block = pl.BlockSpec((groups // steps, depth, LANES), lambda i: (i, 0, 0))
    return pl.pallas_call(
        reorder_kernel,
        grid=(steps,),
        in_specs=[block],
        out_specs=block,
        out_shape=jax.ShapeDtypeStruct(bands.shape, bands.dtype),
        scratch_shapes=[pltpu.VMEM((depth, depth), jnp.bfloat16)],
        name="reorder_tiles",
    )(bands)


def parity_position(lane):
    within = lane % BS
    return 2 * (within % (BS // 2)) + within // (BS // 2)


def spread_matrix(offset):
    row = lax.broadcasted_iota(jnp.int32, (LANES, 2 * LANES), 0)
    col = lax.broadcasted_iota(jnp.int32, (LANES, 2 * LANES), 1)
    lane = col % LANES
    wanted_half = (col // LANES) == (lane // BS)
    hit = wanted_half & (row == parity_position(lane) + offset)
    return hit.astype(jnp.float32).astype(jnp.bfloat16)


def pack_blocks(index_ref, pick_at, low_ref, high_ref, out_ref):
    shards = out_ref.shape[0]
    for shard in range(shards):
        first = index_ref[pick_at + shard]
        second = index_ref[pick_at + shards + shard]
        out_ref[shard] = low_ref[first] + high_ref[second]


def pack_kernel(at, sources, index_hbm, in_ref, out_ref, index_ref, low_ref, high_ref, index_sem):
    tiles, rows = low_ref.shape[0] // 2, low_ref.shape[1]
    chunk = rows // sources
    index_copy = pltpu.make_async_copy(index_hbm.at[pl.ds(at * INDEX_STRIDE, INDEX_STRIDE)], index_ref, index_sem)
    index_copy.start()
    core = lax.axis_index("section") % 2
    for tile in range(tiles):
        span = pl.ds(tile * chunk, chunk)
        value = jnp.concatenate([in_ref[2 * source + core, span].astype(jnp.bfloat16) for source in range(sources)], axis=0)
        for offset in range(2):
            spread = jnp.dot(value, spread_matrix(offset * BS), preferred_element_type=jnp.float32).astype(jnp.bfloat16)
            low_ref[2 * tile + offset] = spread[:, :LANES]
            high_ref[2 * tile + offset] = spread[:, LANES:]
    index_copy.wait()
    pack_blocks(index_ref, PICKS_AT, low_ref, high_ref, out_ref)


def pack_rows(index, rows_in, at, sources, shards, rows, blocks):
    in_vmem = pl.BlockSpec(memory_space=pltpu.VMEM)
    return pl.pallas_call(
        functools.partial(pack_kernel, at, sources),
        in_specs=[pl.BlockSpec(memory_space=pl.ANY), in_vmem],
        out_specs=in_vmem,
        scratch_shapes=[
            pltpu.SMEM((INDEX_STRIDE,), jnp.int32),
            pltpu.VMEM((blocks, rows, LANES), jnp.bfloat16),
            pltpu.VMEM((blocks, rows, LANES), jnp.bfloat16),
            pltpu.SemaphoreType.DMA,
        ],
        out_shape=jax.ShapeDtypeStruct((shards, rows, LANES), jnp.bfloat16),
        compiler_params=pltpu.CompilerParams(vmem_limit_bytes=VMEM_LIMIT),
        name="pack_rows",
    )(index, rows_in)


def layer_kernel(layer, kind, index_hbm, in_ref, tiles_hbm, bias_ref, *refs):
    if kind == "first":
        sent_hbm, *refs = refs
    out_ref, index_ref, tiles_ref, spread_ref, total_ref, low_ref, high_ref, index_sem, tile_sems = refs
    shards, rows, _ = in_ref.shape
    groups = tiles_ref.shape[0]
    tile_slots = groups * GROUP
    blocks = total_ref.shape[1] - 1
    steps = tile_sems.shape[0]
    per_step = groups // steps
    index_copy = pltpu.make_async_copy(index_hbm.at[pl.ds(layer * INDEX_STRIDE, INDEX_STRIDE)], index_ref, index_sem)
    index_copy.start()
    def tile_copy(source, step):
        span = pl.ds(step * per_step, per_step)
        return pltpu.make_async_copy(source.at[span], tiles_ref.at[span], tile_sems.at[step])

    if kind == "first":
        core = lax.axis_index("section") % 2
        for step in range(steps):
            pl.when(core == 0)(tile_copy(tiles_hbm, step).start)
            pl.when(core == 1)(tile_copy(sent_hbm, step).start)
        tiles_of = tiles_hbm
    else:
        tiles_of = tiles_hbm.at[layer]
        for step in range(steps):
            tile_copy(tiles_of, step).start()
    total_ref[...] = jnp.zeros_like(total_ref)
    low = lax.broadcasted_iota(jnp.int32, (rows, LANES), 1) < BS
    for shard in range(shards):
        value = in_ref[shard].astype(jnp.float32)
        turned = pltpu.roll(value, BS, 1)
        spread_ref[0, 2 * shard] = jnp.where(low, value, 0.0).astype(jnp.bfloat16)
        spread_ref[0, 2 * shard + 1] = jnp.where(low, turned, 0.0).astype(jnp.bfloat16)
        spread_ref[1, 2 * shard] = jnp.where(low, 0.0, turned).astype(jnp.bfloat16)
        spread_ref[1, 2 * shard + 1] = jnp.where(low, 0.0, value).astype(jnp.bfloat16)
    index_copy.wait()
    empty = jnp.zeros((rows, LANES), jnp.bfloat16)
    for group in range(groups):
        if group % per_step == 0:
            tile_copy(tiles_of, group // per_step).wait()
        first_tile = group * GROUP
        left = []
        right = []
        for member in range(GROUP):
            pair = member // 2
            value = spread_ref[pair % 2, index_ref[first_tile + member]]
            left.append(value if pair < 2 else empty)
            right.append(value if pair >= 2 else empty)
        gathered = jnp.concatenate([jnp.concatenate(left, axis=0), jnp.concatenate(right, axis=0)], axis=1)
        product = jnp.dot(gathered, tiles_ref[group], preferred_element_type=jnp.float32)
        for member in range(GROUP):
            column = index_ref[tile_slots + first_tile + member]
            total_ref[member % 2, column] += product[member * rows : (member + 1) * rows]

    even = total_ref[0, :blocks].reshape(blocks * rows, LANES)
    odd = total_ref[1, :blocks].reshape(blocks * rows, LANES)
    summed = (even + pltpu.roll(odd, BS, 1)).reshape(blocks, rows, LANES) + bias_ref[layer][:, None, :]
    result = jnp.clip(summed, 0.0, CLAMP_TOP)
    if kind == "inner":
        value = jnp.dot(
            result.astype(jnp.bfloat16).reshape(blocks * rows, LANES),
            spread_matrix(0),
            preferred_element_type=jnp.float32,
        ).astype(jnp.bfloat16)
        low_ref[...] = value[:, :LANES].reshape(blocks, rows, LANES)
        high_ref[...] = value[:, LANES:].reshape(blocks, rows, LANES)
        pack_blocks(index_ref, PICKS_AT, low_ref, high_ref, out_ref)
        return
    low_rows = lax.broadcasted_iota(jnp.int32, (rows, LANES), 1) < BS
    for tile in range(blocks // 2):
        value = jnp.where(low_rows, result[2 * tile], pltpu.roll(result[2 * tile + 1], BS, 1)).astype(out_ref.dtype)
        if kind == "last":
            out_ref[:, tile * LANES : (tile + 1) * LANES] = value
        else:
            chunk = out_ref.shape[1] // (blocks // 2)
            for target in range(out_ref.shape[0]):
                at = target // 2 * chunk
                out_ref[target, tile * chunk : (tile + 1) * chunk] = value[at : at + chunk]


def run_layer(index, incoming, weights, bias, layer, kind, blocks, layers=None, sent=None):
    shards, rows, _ = incoming.shape
    groups, depth = weights.shape[-3:-1]
    steps = 4
    if kind == "first":
        out_shape = (layers, rows // (layers // 2) * blocks // 2, LANES)
    elif kind == "last":
        out_shape = (rows, blocks * BS)
    else:
        out_shape = (shards, rows, LANES)
    in_vmem = pl.BlockSpec(memory_space=pltpu.VMEM)
    anywhere = pl.BlockSpec(memory_space=pl.ANY)
    operands = [index, incoming, weights, bias] + ([sent] if kind == "first" else [])
    return pl.pallas_call(
        functools.partial(layer_kernel, layer, kind),
        in_specs=[anywhere, in_vmem, anywhere, in_vmem, anywhere][: len(operands)],
        out_specs=in_vmem,
        scratch_shapes=[
            pltpu.SMEM((INDEX_STRIDE,), jnp.int32),
            pltpu.VMEM((groups, depth, LANES), jnp.bfloat16),
            pltpu.VMEM((2, 2 * shards, rows, LANES), jnp.bfloat16),
            pltpu.VMEM((2, blocks + 1, rows, LANES), jnp.float32),
            pltpu.VMEM((blocks, rows, LANES), jnp.bfloat16),
            pltpu.VMEM((blocks, rows, LANES), jnp.bfloat16),
            pltpu.SemaphoreType.DMA,
            pltpu.SemaphoreType.DMA((steps,)),
        ],
        out_shape=jax.ShapeDtypeStruct(out_shape, jnp.bfloat16),
        compiler_params=pltpu.CompilerParams(vmem_limit_bytes=VMEM_LIMIT),
        cost_estimate=pl.CostEstimate(flops=2 * groups * GROUP * 2 * rows * depth * LANES, bytes_accessed=3 << 20, transcendentals=0),
        name="layer_step",
    )(*operands)


def plan_routes(tile_row, tile_col, tile_count, own_index, blocks_dev):
    shards = tile_count.shape[0]
    tile_slots = tile_col.shape[0]
    slot_ids = jnp.arange(tile_slots, dtype=jnp.int32)
    rows = tile_row.reshape(shards, tile_slots)
    own_rows = lax.dynamic_index_in_dim(rows, own_index, 0, keepdims=False)
    own_used = slot_ids < tile_count[own_index]
    own_shards = own_rows // blocks_dev
    earlier = (own_shards[None, :] == own_shards[:, None]) & (own_rows[None, :] < own_rows[:, None]) & own_used[None, :]
    rank = jnp.any(earlier, axis=1).astype(jnp.int32)
    slot = jnp.where(own_used, 2 * own_shards + rank, 0)
    column = jnp.where(own_used, tile_col, blocks_dev)
    wanted = (rows // blocks_dev == own_index) & (slot_ids[None, :] < tile_count[:, None])
    local = rows - own_index * blocks_dev
    lowest = jnp.min(jnp.where(wanted, local, blocks_dev - 1), axis=1)
    highest = jnp.max(jnp.where(wanted, local, 0), axis=1)
    return jnp.concatenate([slot, column, lowest, highest, jnp.zeros(INDEX_STRIDE - PICKS_AT - 2 * shards, jnp.int32)])


def body(features, tiles, tile_row, tile_col, tile_count, bias):
    shards = lax.axis_size("neuron")
    layers = lax.axis_size("section")
    own_index = lax.axis_index("neuron")
    rows, width = features.shape
    blocks = width // BS
    tile_slots = tiles.shape[1]
    with jax.named_scope("tile_order"):
        slabs = tiles[0].reshape(tile_slots // GROUP, GROUP, BS * BS // LANES, LANES)
        bands = slabs.transpose(0, 2, 1, 3).reshape(tile_slots // GROUP, GROUP * BS // 2, LANES)
        ordered = reorder_tiles(bands)
    with jax.named_scope("weight_gather"):
        weights = lax.all_gather(ordered, "section", axis=0)
    with jax.named_scope("routes"):
        routes = plan_routes(tile_row[0], tile_col[0], tile_count[0], own_index, blocks)
        tiled = features.astype(jnp.float32).reshape(rows, width // LANES, LANES).transpose(1, 0, 2).reshape(-1, LANES)
        own = jnp.concatenate([tiled, routes.astype(jnp.float32).reshape(-1, LANES), bias[0].reshape(width // LANES, LANES)])
        shared = lax.all_to_all(jnp.broadcast_to(own[None], (layers,) + own.shape), "section", 0, 0, tiled=True)
        index_at = tiled.shape[0]
        index_rows = INDEX_STRIDE // LANES
        pick_rows = PICKS_AT // LANES
        numbers = shared[:, index_at : index_at + index_rows].astype(jnp.int32)
        numbers = jnp.concatenate([numbers[:, :pick_rows], jnp.roll(numbers[:, pick_rows:], -1, axis=0)], axis=1)
        index = numbers.reshape(-1)
        biases = shared[:, index_at + index_rows :].reshape(layers, blocks, BS)
        biases = jnp.pad(biases, ((0, 0), (0, 0), (0, LANES - BS)))
    with jax.named_scope("first_layer"):
        sent = lax.ppermute(ordered, "section", [(source, source + 1) for source in range(0, layers, 2)])
        wide = rows * layers // 2
        outgoing = pack_rows(index, shared, layers - 1, layers // 2, shards, wide, blocks)
        incoming = lax.all_to_all(outgoing, "neuron", 0, 0, tiled=True)
        finished = run_layer(index, incoming, ordered, biases, 0, "first", blocks, layers, sent)
        spread_rows = lax.all_to_all(finished, "section", 0, 0, tiled=True)
    with jax.named_scope("layers"):
        outgoing = pack_rows(index, spread_rows, 0, 1, shards, rows, blocks)
        for layer in range(1, layers):
            incoming = lax.all_to_all(outgoing, "neuron", 0, 0, tiled=True)
            outgoing = run_layer(index, incoming, weights, biases, layer, "last" if layer == layers - 1 else "inner", blocks)
    return outgoing


def solution(mesh):
    in_specs = (
        P("section", "neuron"),
        P("section", "neuron", None),
        P("section", None),
        P("section", "neuron"),
        P("section", None),
        P("section", "neuron"),
    )
    out_specs = P("section", "neuron")
    return jax.shard_map(body, mesh=mesh, in_specs=in_specs, out_specs=out_specs, check_vma=False)
```

time: 306 us -> 257 us (0.84)
  waiting for transfers between devices: 60.9 us -> 35.8 us
  Pallas kernels: 53 us -> 35.1 us
  blocking collectives: 155 us -> 142 us
  starting transfers between devices: 12.9 us -> 24.8 us
  local copies, waits for them, and re-layouts: 6.24 us -> 2.48 us
    all_gather x1, waiting for transfers between devices: 46.8 us -> 0.01 us  [body(): weights = lax.all_gather(ordered, 'section', axis=0)]
    pallas_call x10 -> x11, Pallas kernels: 53 us -> 35.1 us  [the longest x8 27.8 us: run_layer(): pl.pallas_call(functools.partial(layer_kernel, layer, kind), in_specs=[an...]
    all_to_all x1, waiting for transfers between devices: 14.1 us -> 29.5 us  [body(): incoming = lax.all_to_all(outgoing, 'neuron', 0, 0, tiled=True)]
    all_to_all x7, blocking collectives: 142 us -> 129 us  [body(): incoming = lax.all_to_all(outgoing, 'neuron', 0, 0, tiled=True)]
    all_to_all x0 -> x1, starting transfers between devices: none -> 9.35 us  [body(): lax.all_to_all(jnp.broadcast_to(own[None], (layers,) + own.shape), 'secti...]
    all_to_all x0 -> x1, waiting for transfers between devices: none -> 6.26 us  [body(): lax.all_to_all(jnp.broadcast_to(own[None], (layers,) + own.shape), 'secti...]
    unnamed x12 -> x14, local copies, waits for them, and re-layouts: 4.23 us -> 0.81 us
    ppermute x0 -> x1, starting transfers between devices: none -> 3.36 us  [body(): lax.ppermute(ordered, 'section', [(source, source + 1) for source in rang...]
  transfers between devices with their start and end apart: 2 -> 4, of which waited for: 2 -> 2; matrix products, arithmetic and copies ran while one was open for 2% -> 2% of each run, Pallas kernels for 1% -> 3%
where the time goes in v2:
time: 257 us; the launch traced here: 256 us
  blocking collectives  142 us (55%)
  waiting for transfers between devices  35.8 us (14%)
  Pallas kernels  35.1 us (14%)
  starting transfers between devices  24.8 us (10%)
  between operations  13.7 us (5%)
  other arithmetic  2.58 us (1%)
    all_to_all x7, blocking collectives, body(): incoming = lax.all_to_all(outgoing, 'neuron', 0, 0, tiled=True)  129 us
    all_to_all x1, waiting for transfers between devices, body(): incoming = lax.all_to_all(outgoing, 'neuron', 0, 0, tiled=True)  29.5 us
    pallas_call x8, Pallas kernels, run_layer(): pl.pallas_call(functools.partial(layer_kernel, layer, kind), in_specs=[an...  27.8 us
    all_to_all x1, blocking collectives, body(): spread_rows = lax.all_to_all(finished, 'section', 0, 0, tiled=True)  13.1 us
    all_to_all x1, starting transfers between devices, body(): incoming = lax.all_to_all(outgoing, 'neuron', 0, 0, tiled=True)  12.1 us
    all_to_all x1, starting transfers between devices, body(): lax.all_to_all(jnp.broadcast_to(own[None], (layers,) + own.shape), 'secti...  9.35 us
    all_to_all x1, waiting for transfers between devices, body(): lax.all_to_all(jnp.broadcast_to(own[None], (layers,) + own.shape), 'secti...  6.26 us
  transfers between devices with their start and end apart: 4, of which 2 were waited for; matrix products, arithmetic and copies ran while one was open for 2% of the time, Pallas kernels for 3%

profile of v2, /device:TPU:2, one launch (start us, length us, event | category | flops | bytes accessed | tf_op | source)
XLA Modules:
  0.0 256.4 jit_solution(14737501928446444907)
XLA Ops:
  6.5 0.0 all-gather.3.cloned.1.call-start
  6.5 4.8 %reorder_tiles.1.tiles_hbm = bf16[32,256,128]{2,1,0:T(8,128)(2,1)} custom-call(bf16[32,256,128]{2,1,0:T(8,128)(2,1)} %bitcast.29), custom_call_target="tpu_custom_call" | custom-call | tf_op jit(solution)/shard_map/tile_order/reorder_tiles/pallas_call | solution.py:51
  11.3 0.0 copy-start.1
  11.3 0.0 copy-start.2
  11.3 0.0 copy-start.5
  11.3 0.0 copy-start.4
  11.3 0.0 copy-start.3
  11.3 0.0 copy-start
  11.4 0.0 all-gather.3.cloned.1.call-update
  11.4 0.5 broadcast.182
  11.9 0.3 copy-done.1
  12.2 0.8 reduce.3
  13.0 0.0 copy-done.2
  13.1 0.0 copy-done.5
  13.1 0.6 constant_dynamic-slice_fusion.1
  13.7 0.6 iota_compare_fusion.1
  14.4 0.2 and_reduce_fusion
  14.6 0.2 select_reduce_fusion
  14.8 0.0 copy-done.4
  14.8 0.7 add_select_fusion.1
  15.5 0.1 concatenate.13
  15.5 0.0 copy-done.3
  15.6 0.9 broadcast_in_dim.11
  16.4 9.4 %all-to-all-start = ((f32[8,144,128]{2,1,0:T(8,128)}), f32[8,144,128]{2,1,0:T(8,128)S(1)}, u32[]{:S(2)}, u32[]{:S(2)}) async-start(f32[8,144,128]{2,1,0:T(8,128)} %broadcast_in_dim.11), calls=%async_computation | async-start | bytes 1179648 | tf_op jit(solution)/shard_map/routes/all_to_all | solution.py:269
  25.8 0.0 copy-done
  25.8 3.4 %collective-permute-start = (bf16[32,256,128]{2,1,0:T(8,128)(2,1)S(1)}, bf16[32,256,128]{2,1,0:T(8,128)(2,1)}, u32[]{:S(2)}, u32[]{:S(2)}) collective-permute-start(bf16[32,256,128]{2,1,0:T(8,128)(2,1)S(1)} %copy-done), channel_id=1, source_target_pairs={{0,64},{128,192},{256,320},{384,448},{1,65},{129,193},{257,321},{3... | collective-permute-start | bytes 6291464 | tf_op jit(solution)/shard_map/first_layer/ppermute | solution.py:279
  29.1 6.3 %all-to-all-done.in_ref = f32[8,144,128]{2,1,0:T(8,128)S(1)} async-done(((f32[8,144,128]{2,1,0:T(8,128)}), f32[8,144,128]{2,1,0:T(8,128)S(1)}, u32[]{:S(2)}, u32[]{:S(2)}) %all-to-all-start) | async-done | bytes 589856 | tf_op jit(solution)/shard_map/routes/all_to_all | solution.py:269
  35.4 1.8 pack_rows.2
  37.3 12.1 %all-to-all-start.1 = ((bf16[64,64,128]{2,1,0:T(8,128)(2,1)}), bf16[64,64,128]{2,1,0:T(8,128)(2,1)S(1)}, u32[]{:S(2)}, u32[]{:S(2)}) async-start(bf16[64,64,128]{2,1,0:T(8,128)(2,1)} %pack_rows.2), calls=%async_computation.1 | async-start | bytes 2097152 | tf_op jit(solution)/shard_map/first_layer/all_to_all | solution.py:282
  49.4 0.1 reshape.81
  49.4 0.0 collective-permute-done.refs_0_
  49.5 29.5 %all-to-all-done.1.in_ref = bf16[64,64,128]{2,1,0:T(8,128)(2,1)S(1)} async-done(((bf16[64,64,128]{2,1,0:T(8,128)(2,1)}), bf16[64,64,128]{2,1,0:T(8,128)(2,1)S(1)}, u32[]{:S(2)}, u32[]{:S(2)}) %all-to-all-start.1) | async-done | bytes 1048608 | tf_op jit(solution)/shard_map/first_layer/all_to_all | solution.py:282
  79.0 4.1 %layer_step.8 = bf16[8,128,128]{2,1,0:T(8,128)(2,1)S(1)} custom-call(s32[8192]{0:T(1024)S(1)} %add_bitcast_fusion.index_hbm, bf16[64,64,128]{2,1,0:T(8,128)(2,1)S(1)} %all-to-all-done.1.in_ref, bf16[32,256,128]{2,1,0:T(8,128)(2,1)S(1)} %copy-done, f32[8,16,128]{2,1,0:T(8,128)S(1)} %pad.4.bias_ref, bf16[32,256,128]{2,1,0:T(8,128)(2,1)} %collective-permute-done.refs_0_), custom_call_target="tpu_custom_call" | custom-call | flops 2147483648 | bytes 3145728 | tf_op jit(solution)/shard_map/first_layer/layer_step/pallas_call | solution.py:212
  83.1 13.1 %all_to_all.50.in_ref = bf16[8,128,128]{2,1,0:T(8,128)(2,1)S(1)} all-to-all(bf16[8,128,128]{2,1,0:T(8,128)(2,1)S(1)} %layer_step.8), channel_id=1, replica_groups=mesh['section'=8,'neuron'=64] {'section'}, dimensions={0} | all-to-all | bytes 524288 | tf_op jit(solution)/shard_map/first_layer/all_to_all | solution.py:284
  96.2 0.7 pack_rows.3
  96.9 20.9 %all_to_all.51.in_ref = bf16[64,16,128]{2,1,0:T(8,128)(2,1)S(1)} all-to-all(bf16[64,16,128]{2,1,0:T(8,128)(2,1)S(1)} %pack_rows.3), channel_id=1, replica_groups=mesh['section'=8,'neuron'=64] {'neuron'}, dimensions={0} | all-to-all | bytes 524288 | tf_op jit(solution)/shard_map/layers/all_to_all | solution.py:288
  117.8 0.0 all-gather.3.cloned.1.call-done
  117.8 3.3 %layer_step.9 = bf16[64,16,128]{2,1,0:T(8,128)(2,1)S(1)} custom-call(s32[8192]{0:T(1024)S(1)} %add_bitcast_fusion.index_hbm, bf16[64,16,128]{2,1,0:T(8,128)(2,1)S(1)} %all_to_all.51.in_ref, bf16[8,32,256,128]{3,2,1,0:T(8,128)(2,1)} %bitcast.22, f32[8,16,128]{2,1,0:T(8,128)S(1)} %pad.4.bias_ref), custom_call_target="tpu_custom_call" | custom-call | flops 536870912 | bytes 3145728 | tf_op jit(solution)/shard_map/layers/layer_step/pallas_call | solution.py:212
  121.2 19.5 %all_to_all.52.in_ref = bf16[64,16,128]{2,1,0:T(8,128)(2,1)S(1)} all-to-all(bf16[64,16,128]{2,1,0:T(8,128)(2,1)S(1)} %layer_step.9), channel_id=1, replica_groups=mesh['section'=8,'neuron'=64] {'neuron'}, dimensions={0} | all-to-all | bytes 524288 | tf_op jit(solution)/shard_map/layers/all_to_all | solution.py:288
  140.7 3.3 %layer_step.10 = bf16[64,16,128]{2,1,0:T(8,128)(2,1)S(1)} custom-call(s32[8192]{0:T(1024)S(1)} %add_bitcast_fusion.index_hbm, bf16[64,16,128]{2,1,0:T(8,128)(2,1)S(1)} %all_to_all.52.in_ref, bf16[8,32,256,128]{3,2,1,0:T(8,128)(2,1)} %bitcast.23, f32[8,16,128]{2,1,0:T(8,128)S(1)} %pad.4.bias_ref), custom_call_target="tpu_custom_call" | custom-call | flops 536870912 | bytes 3145728 | tf_op jit(solution)/shard_map/layers/layer_step/pallas_call | solution.py:212
  144.0 18.3 %all_to_all.53.in_ref = bf16[64,16,128]{2,1,0:T(8,128)(2,1)S(1)} all-to-all(bf16[64,16,128]{2,1,0:T(8,128)(2,1)S(1)} %layer_step.10), channel_id=1, replica_groups=mesh['section'=8,'neuron'=64] {'neuron'}, dimensions={0} | all-to-all | bytes 524288 | tf_op jit(solution)/shard_map/layers/all_to_all | solution.py:288
  162.4 3.3 %layer_step.11 = bf16[64,16,128]{2,1,0:T(8,128)(2,1)S(1)} custom-call(s32[8192]{0:T(1024)S(1)} %add_bitcast_fusion.index_hbm, bf16[64,16,128]{2,1,0:T(8,128)(2,1)S(1)} %all_to_all.53.in_ref, bf16[8,32,256,128]{3,2,1,0:T(8,128)(2,1)} %bitcast.24, f32[8,16,128]{2,1,0:T(8,128)S(1)} %pad.4.bias_ref), custom_call_target="tpu_custom_call" | custom-call | flops 536870912 | bytes 3145728 | tf_op jit(solution)/shard_map/layers/layer_step/pallas_call | solution.py:212
  165.7 18.0 %all_to_all.54.in_ref = bf16[64,16,128]{2,1,0:T(8,128)(2,1)S(1)} all-to-all(bf16[64,16,128]{2,1,0:T(8,128)(2,1)S(1)} %layer_step.11), channel_id=1, replica_groups=mesh['section'=8,'neuron'=64] {'neuron'}, dimensions={0} | all-to-all | bytes 524288 | tf_op jit(solution)/shard_map/layers/all_to_all | solution.py:288
  183.7 3.3 %layer_step.12 = bf16[64,16,128]{2,1,0:T(8,128)(2,1)S(1)} custom-call(s32[8192]{0:T(1024)S(1)} %add_bitcast_fusion.index_hbm, bf16[64,16,128]{2,1,0:T(8,128)(2,1)S(1)} %all_to_all.54.in_ref, bf16[8,32,256,128]{3,2,1,0:T(8,128)(2,1)} %bitcast.25, f32[8,16,128]{2,1,0:T(8,128)S(1)} %pad.4.bias_ref), custom_call_target="tpu_custom_call" | custom-call | flops 536870912 | bytes 3145728 | tf_op jit(solution)/shard_map/layers/layer_step/pallas_call | solution.py:212
  187.0 17.4 %all_to_all.55.in_ref = bf16[64,16,128]{2,1,0:T(8,128)(2,1)S(1)} all-to-all(bf16[64,16,128]{2,1,0:T(8,128)(2,1)S(1)} %layer_step.12), channel_id=1, replica_groups=mesh['section'=8,'neuron'=64] {'neuron'}, dimensions={0} | all-to-all | bytes 524288 | tf_op jit(solution)/shard_map/layers/all_to_all | solution.py:288
  204.4 3.3 %layer_step.13 = bf16[64,16,128]{2,1,0:T(8,128)(2,1)S(1)} custom-call(s32[8192]{0:T(1024)S(1)} %add_bitcast_fusion.index_hbm, bf16[64,16,128]{2,1,0:T(8,128)(2,1)S(1)} %all_to_all.55.in_ref, bf16[8,32,256,128]{3,2,1,0:T(8,128)(2,1)} %bitcast.26, f32[8,16,128]{2,1,0:T(8,128)S(1)} %pad.4.bias_ref), custom_call_target="tpu_custom_call" | custom-call | flops 536870912 | bytes 3145728 | tf_op jit(solution)/shard_map/layers/layer_step/pallas_call | solution.py:212
  207.8 17.4 %all_to_all.56.in_ref = bf16[64,16,128]{2,1,0:T(8,128)(2,1)S(1)} all-to-all(bf16[64,16,128]{2,1,0:T(8,128)(2,1)S(1)} %layer_step.13), channel_id=1, replica_groups=mesh['section'=8,'neuron'=64] {'neuron'}, dimensions={0} | all-to-all | bytes 524288 | tf_op jit(solution)/shard_map/layers/all_to_all | solution.py:288
  225.2 3.3 %layer_step.14 = bf16[64,16,128]{2,1,0:T(8,128)(2,1)S(1)} custom-call(s32[8192]{0:T(1024)S(1)} %add_bitcast_fusion.index_hbm, bf16[64,16,128]{2,1,0:T(8,128)(2,1)S(1)} %all_to_all.56.in_ref, bf16[8,32,256,128]{3,2,1,0:T(8,128)(2,1)} %bitcast.27, f32[8,16,128]{2,1,0:T(8,128)S(1)} %pad.4.bias_ref), custom_call_target="tpu_custom_call" | custom-call | flops 536870912 | bytes 3145728 | tf_op jit(solution)/shard_map/layers/layer_step/pallas_call | solution.py:212
  228.5 17.4 %all_to_all.57.in_ref = bf16[64,16,128]{2,1,0:T(8,128)(2,1)S(1)} all-to-all(bf16[64,16,128]{2,1,0:T(8,128)(2,1)S(1)} %layer_step.14), channel_id=1, replica_groups=mesh['section'=8,'neuron'=64] {'neuron'}, dimensions={0} | all-to-all | bytes 524288 | tf_op jit(solution)/shard_map/layers/all_to_all | solution.py:288
  245.9 3.7 %layer_step.15 = bf16[16,1024]{1,0:T(8,128)(2,1)} custom-call(s32[8192]{0:T(1024)S(1)} %add_bitcast_fusion.index_hbm, bf16[64,16,128]{2,1,0:T(8,128)(2,1)S(1)} %all_to_all.57.in_ref, bf16[8,32,256,128]{3,2,1,0:T(8,128)(2,1)} %bitcast.28, f32[8,16,128]{2,1,0:T(8,128)S(1)} %pad.4.bias_ref), custom_call_target="tpu_custom_call" | custom-call | flops 536870912 | bytes 3145728 | tf_op jit(solution)/shard_map/layers/layer_step/pallas_call | solution.py:212
  (15 shorter events, 0.1 us)
Async XLA Ops:
  6.5 111.3 %all-gather.3.cloned.1.call-start = ((), (), s32[]{:S(2)}) async-start(), calls=%async_computation.10 | async-start | bytes 18874368 | tf_op jit(solution)/shard_map/weight_gather/all_gather | solution.py:264
  11.3 0.8 copy-start.1
  11.3 1.7 copy-start.2
  11.3 1.7 copy-start.5
  11.3 3.4 %copy-start.4 = (s32[1,256]{1,0:T(1,128)S(1)}, s32[1,256]{1,0:T(1,128)}, u32[]{:S(2)}) copy-start(s32[1,256]{1,0:T(1,128)} %param.9) | copy-start | bytes 3076
  11.3 4.2 %copy-start.3 = (f32[1,1024]{1,0:T(1,128)S(1)}, f32[1,1024]{1,0:T(1,128)}, u32[]{:S(2)}) copy-start(f32[1,1024]{1,0:T(1,128)} %param.11) | copy-start | bytes 12292
  11.3 14.4 %copy-start = (bf16[32,256,128]{2,1,0:T(8,128)(2,1)S(1)}, bf16[32,256,128]{2,1,0:T(8,128)(2,1)}, u32[]{:S(2)}) copy-start(bf16[32,256,128]{2,1,0:T(8,128)(2,1)} %reorder_tiles.1.tiles_hbm) | copy-start | bytes 6291460
  16.4 19.0 %all-to-all-start = ((f32[8,144,128]{2,1,0:T(8,128)}), f32[8,144,128]{2,1,0:T(8,128)S(1)}, u32[]{:S(2)}, u32[]{:S(2)}) async-start(f32[8,144,128]{2,1,0:T(8,128)} %broadcast_in_dim.11), calls=%async_computation | async-start | bytes 1179648 | tf_op jit(solution)/shard_map/routes/all_to_all | solution.py:269
  25.8 23.7 %collective-permute-start = (bf16[32,256,128]{2,1,0:T(8,128)(2,1)S(1)}, bf16[32,256,128]{2,1,0:T(8,128)(2,1)}, u32[]{:S(2)}, u32[]{:S(2)}) collective-permute-start(bf16[32,256,128]{2,1,0:T(8,128)(2,1)S(1)} %copy-done), channel_id=1, source_target_pairs={{0,64},{128,192},{256,320},{384,448},{1,65},{129,193},{257,321},{3... | collective-permute-start | bytes 6291464 | tf_op jit(solution)/shard_map/first_layer/ppermute | solution.py:279
  37.3 41.7 %all-to-all-start.1 = ((bf16[64,64,128]{2,1,0:T(8,128)(2,1)}), bf16[64,64,128]{2,1,0:T(8,128)(2,1)S(1)}, u32[]{:S(2)}, u32[]{:S(2)}) async-start(bf16[64,64,128]{2,1,0:T(8,128)(2,1)} %pack_rows.2), calls=%async_computation.1 | async-start | bytes 2097152 | tf_op jit(solution)/shard_map/first_layer/all_to_all | solution.py:282
Sparse Core Ops, SparseCore 0:
  11.5 97.3 all-gather.2

commit v3 on v2

v3 whole, which is shorter than its diff:
```python
import functools

import jax
import jax.numpy as jnp
from jax import lax
from jax.experimental import pallas as pl
from jax.experimental.pallas import tpu as pltpu
from jax.sharding import PartitionSpec as P

BS = 64
CLAMP_TOP = 32.0
LANES = 128
GROUP = 8
INDEX_STRIDE = 1024
PICKS_AT = 512
VMEM_LIMIT = 44 << 20


def reorder_kernel(in_ref, out_ref, move_ref):
    groups, depth, _ = in_ref.shape
    half = depth // GROUP
    pairs = GROUP // 2

    @pl.when(pl.program_id(0) == 0)
    def _():
        row = lax.broadcasted_iota(jnp.int32, (depth, depth), 0)
        col = lax.broadcasted_iota(jnp.int32, (depth, depth), 1)
        parity = row // (pairs * half)
        pair = row // half % pairs
        slab = row % half
        hit = col == slab * GROUP + 2 * pair + parity
        move_ref[...] = hit.astype(jnp.float32).astype(jnp.bfloat16)

    low = lax.broadcasted_iota(jnp.int32, (half, LANES), 1) < BS
    for group in range(groups):
        moved = jnp.dot(move_ref[...], in_ref[group], preferred_element_type=jnp.float32)
        for pair in range(pairs):
            first = moved[pair * half : (pair + 1) * half]
            second = moved[(pairs + pair) * half : (pairs + pair + 1) * half]
            even = jnp.where(low, first, pltpu.roll(second, BS, 1))
            odd = jnp.where(low, pltpu.roll(first, BS, 1), second)
            at = pair * 2 * half
            out_ref[group, at : at + half, :] = even.astype(out_ref.dtype)
            out_ref[group, at + half : at + 2 * half, :] = odd.astype(out_ref.dtype)


def reorder_tiles(bands):
    groups, depth, _ = bands.shape
    steps = 4
    block = pl.BlockSpec((groups // steps, depth, LANES), lambda i: (i, 0, 0))
    return pl.pallas_call(
        reorder_kernel,
        grid=(steps,),
        in_specs=[block],
        out_specs=block,
        out_shape=jax.ShapeDtypeStruct(bands.shape, bands.dtype),
        scratch_shapes=[pltpu.VMEM((depth, depth), jnp.bfloat16)],
        name="reorder_tiles",
    )(bands)


def parity_position(lane):
    within = lane % BS
    return 2 * (within % (BS // 2)) + within // (BS // 2)


def spread_matrix(offset):
    row = lax.broadcasted_iota(jnp.int32, (LANES, 2 * LANES), 0)
    col = lax.broadcasted_iota(jnp.int32, (LANES, 2 * LANES), 1)
    lane = col % LANES
    wanted_half = (col // LANES) == (lane // BS)
    hit = wanted_half & (row == parity_position(lane) + offset)
    return hit.astype(jnp.float32).astype(jnp.bfloat16)


def pack_blocks(index_ref, picks_at, low_ref, high_ref, out_ref):
    for shard in range(out_ref.shape[0]):
        first = index_ref[picks_at + 2 * shard]
        second = index_ref[picks_at + LANES + 2 * shard]
        out_ref[shard] = low_ref[first] + high_ref[second]


def pack_kernel(at, sources, index_hbm, in_ref, out_ref, index_ref, low_ref, high_ref, index_sem):
    chunk = out_ref.shape[1] // sources
    index_copy = pltpu.make_async_copy(index_hbm.at[pl.ds(at * INDEX_STRIDE, INDEX_STRIDE)], index_ref, index_sem)
    index_copy.start()
    core = lax.axis_index("section") % 2
    matrices = [spread_matrix(offset * BS) for offset in range(2)]
    for tile in range(low_ref.shape[0] // 2):
        span = pl.ds(tile * chunk, chunk)
        value = jnp.concatenate([in_ref[2 * source + core, span] for source in range(sources)], axis=0)
        for offset in range(2):
            spread = jnp.dot(value, matrices[offset], preferred_element_type=jnp.float32).astype(jnp.bfloat16)
            low_ref[2 * tile + offset] = spread[:, :LANES]
            high_ref[2 * tile + offset] = spread[:, LANES:]
    index_copy.wait()
    pack_blocks(index_ref, PICKS_AT, low_ref, high_ref, out_ref)


def pack_rows(index, rows_in, at, sources, shards, rows, blocks):
    in_vmem = pl.BlockSpec(memory_space=pltpu.VMEM)
    return pl.pallas_call(
        functools.partial(pack_kernel, at, sources),
        in_specs=[pl.BlockSpec(memory_space=pl.ANY), in_vmem],
        out_specs=in_vmem,
        scratch_shapes=[
            pltpu.SMEM((INDEX_STRIDE,), jnp.int32),
            pltpu.VMEM((blocks, rows, LANES), jnp.bfloat16),
            pltpu.VMEM((blocks, rows, LANES), jnp.bfloat16),
            pltpu.SemaphoreType.DMA,
        ],
        out_shape=jax.ShapeDtypeStruct((shards, rows, LANES), jnp.bfloat16),
        compiler_params=pltpu.CompilerParams(vmem_limit_bytes=VMEM_LIMIT),
        name="pack_rows",
    )(index, rows_in)


def layer_kernel(layer, kind, fetch, ahead, *refs):
    refs = list(refs)
    index_hbm, in_ref, bias_ref = (refs.pop(0) for _ in range(3))
    given_ref = None if fetch else refs.pop(0)
    sent_hbm = refs.pop(0) if kind == "first" else None
    weights_hbm = refs.pop(0) if fetch or ahead else None
    out_ref = refs.pop(0)
    next_ref = refs.pop(0) if ahead else None
    index_ref, fetched_ref, spread_ref, low_ref, high_ref, index_sem, tile_sems, next_sem, *total_refs = refs
    tiles_ref = fetched_ref if fetch else given_ref
    shards, rows, _ = in_ref.shape
    groups = tiles_ref.shape[0]
    tile_slots = groups * GROUP
    blocks = total_refs[0].shape[0] - 1
    steps = tile_sems.shape[0]
    per_step = groups // steps
    index_copy = pltpu.make_async_copy(
        index_hbm.at[pl.ds(layer * INDEX_STRIDE, index_ref.shape[0])], index_ref, index_sem
    )
    index_copy.start()

    def tile_copy(source, step):
        span = pl.ds(step * per_step, per_step)
        return pltpu.make_async_copy(source.at[span], fetched_ref.at[span], tile_sems.at[step])

    if kind == "first":
        core = lax.axis_index("section") % 2
        tiles_hbm = weights_hbm
        for step in range(steps):
            pl.when(core == 0)(tile_copy(tiles_hbm, step).start)
            pl.when(core == 1)(tile_copy(sent_hbm, step).start)
    elif fetch:
        tiles_hbm = weights_hbm.at[layer]
        for step in range(steps):
            tile_copy(tiles_hbm, step).start()
    if ahead:
        next_copy = pltpu.make_async_copy(weights_hbm.at[layer + 1], next_ref, next_sem)
        next_copy.start()
    for total_ref in total_refs:
        total_ref[...] = jnp.zeros_like(total_ref)
    low = lax.broadcasted_iota(jnp.int32, (rows, LANES), 1) < BS
    for shard in range(shards):
        value = in_ref[shard].astype(jnp.float32)
        turned = pltpu.roll(value, BS, 1)
        spread_ref[0, 2 * shard] = jnp.where(low, value, 0.0).astype(jnp.bfloat16)
        spread_ref[0, 2 * shard + 1] = jnp.where(low, turned, 0.0).astype(jnp.bfloat16)
        spread_ref[1, 2 * shard] = jnp.where(low, 0.0, turned).astype(jnp.bfloat16)
        spread_ref[1, 2 * shard + 1] = jnp.where(low, 0.0, value).astype(jnp.bfloat16)
    index_copy.wait()
    empty = jnp.zeros((rows, LANES), jnp.bfloat16)
    for group in range(groups):
        if fetch and group % per_step == 0:
            tile_copy(tiles_hbm, group // per_step).wait()
        first_tile = group * GROUP
        left = []
        right = []
        for member in range(GROUP):
            pair = member // 2
            value = spread_ref[pair % 2, index_ref[first_tile + member]]
            left.append(value if pair < 2 else empty)
            right.append(value if pair >= 2 else empty)
        gathered = jnp.concatenate([jnp.concatenate(left, axis=0), jnp.concatenate(right, axis=0)], axis=1)
        product = jnp.dot(gathered, tiles_ref[group], preferred_element_type=jnp.float32)
        for member in range(GROUP):
            column = index_ref[tile_slots + first_tile + member]
            total_refs[member][column] += product[member * rows : (member + 1) * rows]

    even, odd = (
        sum(total_refs[member][:blocks] for member in range(parity, GROUP, 2)).reshape(blocks * rows, LANES)
        for parity in range(2)
    )
    summed = (even + pltpu.roll(odd, BS, 1)).reshape(blocks, rows, LANES) + bias_ref[layer][:, None, :]
    result = jnp.clip(summed, 0.0, CLAMP_TOP)
    if kind == "inner":
        value = jnp.dot(
            result.astype(jnp.bfloat16).reshape(blocks * rows, LANES),
            spread_matrix(0),
            preferred_element_type=jnp.float32,
        ).astype(jnp.bfloat16)
        low_ref[...] = value[:, :LANES].reshape(blocks, rows, LANES)
        high_ref[...] = value[:, LANES:].reshape(blocks, rows, LANES)
        pack_blocks(index_ref, INDEX_STRIDE + PICKS_AT, low_ref, high_ref, out_ref)
        if ahead:
            next_copy.wait()
        return
    low_rows = lax.broadcasted_iota(jnp.int32, (rows, LANES), 1) < BS
    for tile in range(blocks // 2):
        value = jnp.where(low_rows, result[2 * tile], pltpu.roll(result[2 * tile + 1], BS, 1)).astype(out_ref.dtype)
        if kind == "last":
            out_ref[:, tile * LANES : (tile + 1) * LANES] = value
        else:
            chunk = out_ref.shape[1] // (blocks // 2)
            for target in range(out_ref.shape[0]):
                at = target // 2 * chunk
                out_ref[target, tile * chunk : (tile + 1) * chunk] = value[at : at + chunk]


def run_layer(index, incoming, bias, layer, kind, blocks, layers, weights=None, given=None, sent=None):
    shards, rows, _ = incoming.shape
    fetch = given is None
    ahead = kind == "inner"
    groups, depth = (weights if fetch else given).shape[-3:-1]
    steps = 4
    if kind == "first":
        out_shape = (layers, rows // (layers // 2) * blocks // 2, LANES)
    elif kind == "last":
        out_shape = (rows, blocks * BS)
    else:
        out_shape = (shards, rows, LANES)
    in_vmem = pl.BlockSpec(memory_space=pltpu.VMEM)
    anywhere = pl.BlockSpec(memory_space=pl.ANY)
    operands = [(index, anywhere), (incoming, in_vmem), (bias, in_vmem)]
    if not fetch:
        operands.append((given, in_vmem))
    if kind == "first":
        operands.append((sent, anywhere))
    if fetch or ahead:
        operands.append((weights, anywhere))
    results = [jax.ShapeDtypeStruct(out_shape, jnp.bfloat16)]
    if ahead:
        results.append(jax.ShapeDtypeStruct((groups, depth, LANES), jnp.bfloat16))
    done = pl.pallas_call(
        functools.partial(layer_kernel, layer, kind, fetch, ahead),
        in_specs=[spec for _, spec in operands],
        out_specs=[in_vmem] * len(results),
        scratch_shapes=[
            pltpu.SMEM((2 * INDEX_STRIDE if kind == "inner" else INDEX_STRIDE,), jnp.int32),
            pltpu.VMEM((groups if fetch else 1, depth, LANES), jnp.bfloat16),
            pltpu.VMEM((2, 2 * shards, rows, LANES), jnp.bfloat16),
            pltpu.VMEM((blocks, rows, LANES), jnp.bfloat16),
            pltpu.VMEM((blocks, rows, LANES), jnp.bfloat16),
            pltpu.SemaphoreType.DMA,
            pltpu.SemaphoreType.DMA((steps,)),
            pltpu.SemaphoreType.DMA,
        ]
        + [pltpu.VMEM((blocks + 1, rows, LANES), jnp.float32)] * GROUP,
        out_shape=results,
        compiler_params=pltpu.CompilerParams(vmem_limit_bytes=VMEM_LIMIT),
        cost_estimate=pl.CostEstimate(flops=2 * groups * GROUP * 2 * rows * depth * LANES, bytes_accessed=3 << 20, transcendentals=0),
        name="layer_step",
    )(*[operand for operand, _ in operands])
    return done if ahead else done[0]


def plan_kernel(blocks_dev, count_ref, rows_ref, cols_ref, counts_ref, bias_ref, in_ref, out_ref):
    own = lax.axis_index("neuron")
    per_shard = cols_ref.shape[0]
    lane = lax.broadcasted_iota(jnp.int32, (LANES, LANES), 1)
    sub = lax.broadcasted_iota(jnp.int32, (LANES, LANES), 0)
    unused = 1 << 16
    own_rows = rows_ref[pl.ds(own * per_shard, per_shard), :]
    slot_ids = lax.broadcasted_iota(jnp.int32, (per_shard, LANES), 0) * LANES + lax.broadcasted_iota(
        jnp.int32, (per_shard, LANES), 1
    )
    used = slot_ids < count_ref[own]
    known = jnp.where(used, own_rows, unused)
    across = [jnp.broadcast_to(own_rows[half : half + 1], (LANES, LANES)) for half in range(per_shard)]
    down = [
        jnp.broadcast_to(known[half : half + 1].astype(jnp.float32), (LANES, LANES)).T.astype(jnp.int32)
        for half in range(per_shard)
    ]
    ranks = []
    for here in across:
        earlier = jnp.zeros((1, LANES), jnp.int32)
        for there in down:
            hit = (there // blocks_dev == here // blocks_dev) & (there < here)
            earlier = jnp.maximum(earlier, jnp.max(hit.astype(jnp.int32), axis=0, keepdims=True))
        ranks.append(earlier)
    rank = jnp.concatenate(ranks, axis=0)
    slot = jnp.where(used, 2 * (own_rows // blocks_dev) + rank, 0)
    column = jnp.where(used, cols_ref[...], blocks_dev)
    counts = jnp.sum(
        jnp.where(lane == sub // per_shard, jnp.broadcast_to(counts_ref[...], (LANES, LANES)), 0).astype(jnp.float32),
        axis=1,
        keepdims=True,
    ).astype(jnp.int32)
    rows = rows_ref[...]
    wanted = (rows // blocks_dev == own) & ((sub % per_shard) * LANES + lane < counts)
    local = rows - own * blocks_dev
    lowest = jnp.min(jnp.where(wanted, local, blocks_dev - 1).astype(jnp.float32), axis=1, keepdims=True)
    highest = jnp.max(jnp.where(wanted, local, 0).astype(jnp.float32), axis=1, keepdims=True)
    lowest = jnp.broadcast_to(lowest, (LANES, LANES)).T[:8]
    highest = jnp.broadcast_to(highest, (LANES, LANES)).T[:8]
    lowest = jnp.minimum(lowest, pltpu.roll(lowest, LANES - 1, 1))
    highest = jnp.maximum(highest, pltpu.roll(highest, LANES - 1, 1))
    numbers = [slot.astype(jnp.float32), column.astype(jnp.float32), lowest[:1], highest[:1]]
    numbers.append(jnp.zeros((14 - 2 * per_shard, LANES), jnp.float32))
    bias = bias_ref[...]
    rounded = bias.astype(jnp.bfloat16)
    rest = bias - rounded.astype(jnp.float32)
    rest_rounded = rest.astype(jnp.bfloat16)
    last = (rest - rest_rounded.astype(jnp.float32)).astype(jnp.bfloat16)
    small = jnp.concatenate(numbers, axis=0).astype(jnp.bfloat16)
    parts = jnp.concatenate([rounded.astype(jnp.float32), rest_rounded.astype(jnp.float32)], axis=0).astype(jnp.bfloat16)
    ends = jnp.concatenate([last.astype(jnp.float32), jnp.zeros_like(bias)], axis=0).astype(jnp.bfloat16)
    rows_in, width = in_ref.shape
    for target in range(out_ref.shape[0]):
        for tile in range(width // LANES):
            out_ref[target, tile * rows_in : (tile + 1) * rows_in] = in_ref[:, tile * LANES : (tile + 1) * LANES]
        at = rows_in * width // LANES
        for piece in (small, parts, ends):
            out_ref[target, at : at + piece.shape[0]] = piece
            at += piece.shape[0]


def plan_routes(tile_row, tile_col, tile_count, bias, features, blocks_dev, layers):
    shards = tile_count.shape[1]
    rows, width = features.shape
    in_vmem = pl.BlockSpec(memory_space=pltpu.VMEM)
    counts = jnp.pad(tile_count, ((0, 0), (0, LANES - shards)))
    return pl.pallas_call(
        functools.partial(plan_kernel, blocks_dev),
        in_specs=[pl.BlockSpec(memory_space=pltpu.SMEM)] + [in_vmem] * 5,
        out_specs=in_vmem,
        out_shape=jax.ShapeDtypeStruct((layers, rows * width // LANES + 48, LANES), jnp.bfloat16),
        cost_estimate=pl.CostEstimate(flops=0, bytes_accessed=4 << 20, transcendentals=0),
        name="plan_routes",
    )(
        tile_count[0],
        tile_row.reshape(-1, LANES),
        tile_col.reshape(-1, LANES),
        counts,
        bias.reshape(-1, LANES),
        features,
    )


def body(features, tiles, tile_row, tile_col, tile_count, bias):
    shards = lax.axis_size("neuron")
    layers = lax.axis_size("section")
    rows, width = features.shape
    blocks = width // BS
    tile_slots = tiles.shape[1]
    to_odd = [(source, source + 1) for source in range(0, layers, 2)]
    with jax.named_scope("tile_order"):
        slabs = tiles[0].reshape(tile_slots // GROUP, GROUP, BS * BS // LANES, LANES)
        bands = slabs.transpose(0, 2, 1, 3).reshape(tile_slots // GROUP, GROUP * BS // 2, LANES)
        ordered = reorder_tiles(bands)
    with jax.named_scope("weight_gather"):
        weights = lax.all_gather(ordered, "section", axis=0)
    with jax.named_scope("routes"):
        plan = plan_routes(tile_row, tile_col, tile_count, bias, features, blocks, layers)
        shared = lax.all_to_all(plan, "section", 0, 0, tiled=True)
        at = rows * width // LANES
        index = shared[:, at : at + 8].astype(jnp.int32).reshape(-1)
        parts = [shared[:, at + start : at + start + 8].astype(jnp.float32) for start in (16, 24, 32)]
        biases = (parts[0] + parts[1] + parts[2]).reshape(layers, blocks, BS)
        biases = jnp.pad(biases, ((0, 0), (0, 0), (0, LANES - BS)))
    with jax.named_scope("first_layer"):
        sent = lax.ppermute(ordered, "section", to_odd)
        outgoing = pack_rows(index, shared, 0, layers // 2, shards, rows * layers // 2, blocks)
        incoming = lax.all_to_all(outgoing, "neuron", 0, 0, tiled=True)
        finished = run_layer(index, incoming, biases, 0, "first", blocks, layers, weights=ordered, sent=sent)
        own_rows = lax.all_to_all(finished, "section", 0, 0, tiled=True)
    with jax.named_scope("layers"):
        outgoing = pack_rows(index, own_rows, 1, 1, shards, rows, blocks)
        given = None
        for layer in range(1, layers - 1):
            incoming = lax.all_to_all(outgoing, "neuron", 0, 0, tiled=True)
            outgoing, given = run_layer(index, incoming, biases, layer, "inner", blocks, layers, weights, given)
        incoming = lax.all_to_all(outgoing, "neuron", 0, 0, tiled=True)
        return run_layer(index, incoming, biases, layers - 1, "last", blocks, layers, given=given)


def solution(mesh):
    in_specs = (
        P("section", "neuron"),
        P("section", "neuron", None),
        P("section", None),
        P("section", "neuron"),
        P("section", None),
        P("section", "neuron"),
    )
    out_specs = P("section", "neuron")
    return jax.shard_map(body, mesh=mesh, in_specs=in_specs, out_specs=out_specs, check_vma=False)
```

time: 257 us -> 248 us (0.965)
  Pallas kernels: 35.1 us -> 29.2 us
  blocking collectives: 142 us -> 145 us
  waiting for transfers between devices: 35.8 us -> 33.2 us
    pallas_call x8 -> x9, Pallas kernels: 27.8 us -> 21.8 us  [the longest x8 19.8 us: run_layer(): pl.pallas_call(functools.partial(layer_kernel, layer, kind, fetch, ahead)...]
    all_to_all x7, blocking collectives: 129 us -> 132 us  [body(): incoming = lax.all_to_all(outgoing, 'neuron', 0, 0, tiled=True)]
  transfers between devices with their start and end apart: 4 -> 4, of which waited for: 2 -> 2; matrix products, arithmetic and copies ran while one was open for 2% -> 0% of each run, Pallas kernels for 3% -> 4%
where the time goes in v3:
time: 248 us; the launch traced here: 247 us
  blocking collectives  145 us (58%)
  waiting for transfers between devices  33.2 us (13%)
  Pallas kernels  29.2 us (12%)
  starting transfers between devices  25 us (10%)
  between operations  13.5 us (5%)
    all_to_all x7, blocking collectives, body(): incoming = lax.all_to_all(outgoing, 'neuron', 0, 0, tiled=True)  132 us
    all_to_all x1, waiting for transfers between devices, body(): incoming = lax.all_to_all(outgoing, 'neuron', 0, 0, tiled=True)  29.4 us
    pallas_call x8, Pallas kernels, run_layer(): pl.pallas_call(functools.partial(layer_kernel, layer, kind, fetch, ahead)...  19.8 us
    all_to_all x1, blocking collectives, body(): own_rows = lax.all_to_all(finished, 'section', 0, 0, tiled=True)  13.1 us
    all_to_all x1, starting transfers between devices, body(): incoming = lax.all_to_all(outgoing, 'neuron', 0, 0, tiled=True)  12.4 us
    all_to_all x1, starting transfers between devices, body(): shared = lax.all_to_all(plan, 'section', 0, 0, tiled=True)  9.26 us
  transfers between devices with their start and end apart: 4, of which 2 were waited for; matrix products, arithmetic and copies ran while one was open for 0% of the time, Pallas kernels for 4%

profile of v3, /device:TPU:2, one launch (start us, length us, event | category | flops | bytes accessed | tf_op | source)
XLA Modules:
  0.0 247.1 jit_solution(1219335265765118851)
XLA Ops:
  6.5 0.0 all-gather.3.cloned.1.call-start
  6.5 4.8 %reorder_tiles.1.refs_4_ = bf16[32,256,128]{2,1,0:T(8,128)(2,1)} custom-call(bf16[32,256,128]{2,1,0:T(8,128)(2,1)} %bitcast.21), custom_call_target="tpu_custom_call" | custom-call | tf_op jit(solution)/shard_map/tile_order/reorder_tiles/pallas_call | solution.py:51
  11.3 0.0 copy-start.1
  11.3 0.0 copy-start
  11.3 0.0 all-gather.3.cloned.1.call-update
  11.3 0.6 copy-done.1
  12.0 0.5 pad.8.counts_ref
  12.5 2.0 plan_routes.1
  14.5 9.3 %all-to-all-start = ((bf16[8,176,128]{2,1,0:T(8,128)(2,1)}), bf16[8,176,128]{2,1,0:T(8,128)(2,1)S(1)}, u32[]{:S(2)}, u32[]{:S(2)}) async-start(bf16[8,176,128]{2,1,0:T(8,128)(2,1)} %plan_routes.1), calls=%async_computation | async-start | bytes 720896 | tf_op jit(solution)/shard_map/routes/all_to_all | solution.py:360
  23.7 0.0 copy-done
  23.7 3.4 %collective-permute-start = (bf16[32,256,128]{2,1,0:T(8,128)(2,1)S(1)}, bf16[32,256,128]{2,1,0:T(8,128)(2,1)}, u32[]{:S(2)}, u32[]{:S(2)}) collective-permute-start(bf16[32,256,128]{2,1,0:T(8,128)(2,1)S(1)} %copy-done), channel_id=1, source_target_pairs={{0,64},{128,192},{256,320},{384,448},{1,65},{129,193},{257,321},{3... | collective-permute-start | bytes 6291464 | tf_op jit(solution)/shard_map/first_layer/ppermute | solution.py:367
  27.1 3.8 %all-to-all-done.in_ref = bf16[8,176,128]{2,1,0:T(8,128)(2,1)S(1)} async-done(((bf16[8,176,128]{2,1,0:T(8,128)(2,1)}), bf16[8,176,128]{2,1,0:T(8,128)(2,1)S(1)}, u32[]{:S(2)}, u32[]{:S(2)}) %all-to-all-start) | async-done | bytes 360480 | tf_op jit(solution)/shard_map/routes/all_to_all | solution.py:360
  30.9 1.9 pack_rows.2
  32.8 12.4 %all-to-all-start.1 = ((bf16[64,64,128]{2,1,0:T(8,128)(2,1)}), bf16[64,64,128]{2,1,0:T(8,128)(2,1)}, u32[]{:S(2)}, u32[]{:S(2)}) async-start(bf16[64,64,128]{2,1,0:T(8,128)(2,1)} %pack_rows.2), calls=%async_computation.1 | async-start | bytes 2097152 | tf_op jit(solution)/shard_map/first_layer/all_to_all | solution.py:369
  45.2 0.1 reshape.25
  45.3 0.0 collective-permute-done.refs_3_
  45.3 29.4 %all-to-all-done.1.refs_1_ = bf16[64,64,128]{2,1,0:T(8,128)(2,1)} async-done(((bf16[64,64,128]{2,1,0:T(8,128)(2,1)}), bf16[64,64,128]{2,1,0:T(8,128)(2,1)}, u32[]{:S(2)}, u32[]{:S(2)}) %all-to-all-start.1) | async-done | bytes 1048608 | tf_op jit(solution)/shard_map/first_layer/all_to_all | solution.py:369
  74.7 5.5 %layer_step.8 = bf16[8,128,128]{2,1,0:T(8,128)(2,1)S(1)} custom-call(s32[8192]{0:T(1024)S(1)} %fusion.index_hbm.refs_0_, bf16[64,64,128]{2,1,0:T(8,128)(2,1)} %all-to-all-done.1.refs_1_, f32[8,16,128]{2,1,0:T(8,128)S(1)} %pad.9.refs_2_, bf16[32,256,128]{2,1,0:T(8,128)(2,1)} %collective-permute-done.refs_3_, bf16[32,256,128]{2,1,0:T(8,128)(2,1)S(1)} %copy-done), custom_call_target="tpu_custom_call" | custom-call | flops 2147483648 | bytes 3145728 | tf_op jit(solution)/shard_map/first_layer/layer_step/pallas_call | solution.py:239
  80.2 13.1 %all_to_all.50.in_ref = bf16[8,128,128]{2,1,0:T(8,128)(2,1)S(1)} all-to-all(bf16[8,128,128]{2,1,0:T(8,128)(2,1)S(1)} %layer_step.8), channel_id=1, replica_groups=mesh['section'=8,'neuron'=64] {'section'}, dimensions={0} | all-to-all | bytes 524288 | tf_op jit(solution)/shard_map/first_layer/all_to_all | solution.py:371
  93.3 0.7 pack_rows.3
  94.0 20.9 %all_to_all.51.refs_1_ = bf16[64,16,128]{2,1,0:T(8,128)(2,1)S(1)} all-to-all(bf16[64,16,128]{2,1,0:T(8,128)(2,1)S(1)} %pack_rows.3), channel_id=1, replica_groups=mesh['section'=8,'neuron'=64] {'neuron'}, dimensions={0} | all-to-all | bytes 524288 | tf_op jit(solution)/shard_map/layers/all_to_all | solution.py:376
  114.9 0.0 all-gather.3.cloned.1.call-done
  114.9 2.8 %layer_step.9 = (bf16[64,16,128]{2,1,0:T(8,128)(2,1)S(1)}, bf16[32,256,128]{2,1,0:T(8,128)(2,1)S(1)}) custom-call(s32[8192]{0:T(1024)S(1)} %fusion.index_hbm.refs_0_, bf16[64,16,128]{2,1,0:T(8,128)(2,1)S(1)} %all_to_all.51.refs_1_, f32[8,16,128]{2,1,0:T(8,128)S(1)} %pad.9.refs_2_, bf16[8,32,256,128]{3,2,1,0:T(8,128)(2,1)} %bitcast.15), custom_call_target="tpu_custom_call" | custom-call | flops 536870912 | bytes 3145728 | tf_op jit(solution)/shard_map/layers/layer_step/pallas_call | solution.py:239
  117.7 22.4 %all_to_all.52.refs_1_ = bf16[64,16,128]{2,1,0:T(8,128)(2,1)S(1)} all-to-all(bf16[64,16,128]{2,1,0:T(8,128)(2,1)S(1)} %get-tuple-element.17), channel_id=1, replica_groups=mesh['section'=8,'neuron'=64] {'neuron'}, dimensions={0} | all-to-all | bytes 524288 | tf_op jit(solution)/shard_map/layers/all_to_all | solution.py:376
  140.1 1.9 layer_step.10
  142.0 18.3 %all_to_all.53.refs_1_ = bf16[64,16,128]{2,1,0:T(8,128)(2,1)S(1)} all-to-all(bf16[64,16,128]{2,1,0:T(8,128)(2,1)S(1)} %get-tuple-element.19), channel_id=1, replica_groups=mesh['section'=8,'neuron'=64] {'neuron'}, dimensions={0} | all-to-all | bytes 524288 | tf_op jit(solution)/shard_map/layers/all_to_all | solution.py:376
  160.2 1.9 layer_step.11
  162.1 17.9 %all_to_all.54.refs_1_ = bf16[64,16,128]{2,1,0:T(8,128)(2,1)S(1)} all-to-all(bf16[64,16,128]{2,1,0:T(8,128)(2,1)S(1)} %get-tuple-element.21), channel_id=1, replica_groups=mesh['section'=8,'neuron'=64] {'neuron'}, dimensions={0} | all-to-all | bytes 524288 | tf_op jit(solution)/shard_map/layers/all_to_all | solution.py:376
  180.1 1.8 layer_step.12
  181.9 17.5 %all_to_all.55.refs_1_ = bf16[64,16,128]{2,1,0:T(8,128)(2,1)S(1)} all-to-all(bf16[64,16,128]{2,1,0:T(8,128)(2,1)S(1)} %get-tuple-element.23), channel_id=1, replica_groups=mesh['section'=8,'neuron'=64] {'neuron'}, dimensions={0} | all-to-all | bytes 524288 | tf_op jit(solution)/shard_map/layers/all_to_all | solution.py:376
  199.5 1.9 layer_step.13
  201.3 17.4 %all_to_all.56.refs_1_ = bf16[64,16,128]{2,1,0:T(8,128)(2,1)S(1)} all-to-all(bf16[64,16,128]{2,1,0:T(8,128)(2,1)S(1)} %get-tuple-element.25), channel_id=1, replica_groups=mesh['section'=8,'neuron'=64] {'neuron'}, dimensions={0} | all-to-all | bytes 524288 | tf_op jit(solution)/shard_map/layers/all_to_all | solution.py:376
  218.7 1.8 layer_step.14
  220.6 17.4 %all_to_all.57.refs_1_ = bf16[64,16,128]{2,1,0:T(8,128)(2,1)S(1)} all-to-all(bf16[64,16,128]{2,1,0:T(8,128)(2,1)S(1)} %get-tuple-element.27), channel_id=1, replica_groups=mesh['section'=8,'neuron'=64] {'neuron'}, dimensions={0} | all-to-all | bytes 524288 | tf_op jit(solution)/shard_map/layers/all_to_all | solution.py:378
  238.0 2.2 layer_step.15
  (3 shorter events, 0.0 us)
Async XLA Ops:
  6.5 108.4 %all-gather.3.cloned.1.call-start = ((), (), s32[]{:S(2)}) async-start(), calls=%async_computation.10 | async-start | bytes 18874368 | tf_op jit(solution)/shard_map/weight_gather/all_gather | solution.py:357
  11.3 0.7 copy-start.1
  11.3 12.4 %copy-start = (bf16[32,256,128]{2,1,0:T(8,128)(2,1)S(1)}, bf16[32,256,128]{2,1,0:T(8,128)(2,1)}, u32[]{:S(2)}) copy-start(bf16[32,256,128]{2,1,0:T(8,128)(2,1)} %reorder_tiles.1.refs_4_) | copy-start | bytes 6291460
  14.5 16.4 %all-to-all-start = ((bf16[8,176,128]{2,1,0:T(8,128)(2,1)}), bf16[8,176,128]{2,1,0:T(8,128)(2,1)S(1)}, u32[]{:S(2)}, u32[]{:S(2)}) async-start(bf16[8,176,128]{2,1,0:T(8,128)(2,1)} %plan_routes.1), calls=%async_computation | async-start | bytes 720896 | tf_op jit(solution)/shard_map/routes/all_to_all | solution.py:360
  23.7 21.6 %collective-permute-start = (bf16[32,256,128]{2,1,0:T(8,128)(2,1)S(1)}, bf16[32,256,128]{2,1,0:T(8,128)(2,1)}, u32[]{:S(2)}, u32[]{:S(2)}) collective-permute-start(bf16[32,256,128]{2,1,0:T(8,128)(2,1)S(1)} %copy-done), channel_id=1, source_target_pairs={{0,64},{128,192},{256,320},{384,448},{1,65},{129,193},{257,321},{3... | collective-permute-start | bytes 6291464 | tf_op jit(solution)/shard_map/first_layer/ppermute | solution.py:367
  32.8 41.9 %all-to-all-start.1 = ((bf16[64,64,128]{2,1,0:T(8,128)(2,1)}), bf16[64,64,128]{2,1,0:T(8,128)(2,1)}, u32[]{:S(2)}, u32[]{:S(2)}) async-start(bf16[64,64,128]{2,1,0:T(8,128)(2,1)} %pack_rows.2), calls=%async_computation.1 | async-start | bytes 2097152 | tf_op jit(solution)/shard_map/first_layer/all_to_all | solution.py:369
Sparse Core Ops, SparseCore 0:
  11.5 97.3 all-gather.2

commit v4 on v3

--- a/solution.py
+++ b/solution.py
@@ -16,45 +16,56 @@
 VMEM_LIMIT = 44 << 20
 
 
-def reorder_kernel(in_ref, out_ref, move_ref):
+def reorder_kernel(in_hbm, out_hbm, in_ref, out_ref, in_sems, out_sems):
     groups, depth, _ = in_ref.shape
     half = depth // GROUP
     pairs = GROUP // 2
-
-    @pl.when(pl.program_id(0) == 0)
-    def _():
-        row = lax.broadcasted_iota(jnp.int32, (depth, depth), 0)
-        col = lax.broadcasted_iota(jnp.int32, (depth, depth), 1)
-        parity = row // (pairs * half)
-        pair = row // half % pairs
-        slab = row % half
-        hit = col == slab * GROUP + 2 * pair + parity
-        move_ref[...] = hit.astype(jnp.float32).astype(jnp.bfloat16)
-
+    steps = in_sems.shape[0]
+    per_step = groups // steps
+    spans = [pl.ds(step * per_step, per_step) for step in range(steps)]
+    arrivals = [pltpu.make_async_copy(in_hbm.at[span], in_ref.at[span], in_sems.at[step]) for step, span in enumerate(spans)]
+    leaves = [pltpu.make_async_copy(out_ref.at[span], out_hbm.at[span], out_sems.at[step]) for step, span in enumerate(spans)]
+    for copy in arrivals:
+        copy.start()
+    row = lax.broadcasted_iota(jnp.int32, (depth, depth), 0)
+    col = lax.broadcasted_iota(jnp.int32, (depth, depth), 1)
+    parity = row // (pairs * half)
+    pair = row // half % pairs
+    slab = row % half
+    move = (col == slab * GROUP + 2 * pair + parity).astype(jnp.float32).astype(jnp.bfloat16)
     low = lax.broadcasted_iota(jnp.int32, (half, LANES), 1) < BS
-    for group in range(groups):
-        moved = jnp.dot(move_ref[...], in_ref[group], preferred_element_type=jnp.float32)
-        for pair in range(pairs):
-            first = moved[pair * half : (pair + 1) * half]
-            second = moved[(pairs + pair) * half : (pairs + pair + 1) * half]
-            even = jnp.where(low, first, pltpu.roll(second, BS, 1))
-            odd = jnp.where(low, pltpu.roll(first, BS, 1), second)
-            at = pair * 2 * half
-            out_ref[group, at : at + half, :] = even.astype(out_ref.dtype)
-            out_ref[group, at + half : at + 2 * half, :] = odd.astype(out_ref.dtype)
+    for step in range(steps):
+        arrivals[step].wait()
+        for group in range(step * per_step, (step + 1) * per_step):
+            moved = jnp.dot(move, in_ref[group], preferred_element_type=jnp.float32)
+            for pair in range(pairs):
+                first = moved[pair * half : (pair + 1) * half]
+                second = moved[(pairs + pair) * half : (pairs + pair + 1) * half]
+                even = jnp.where(low, first, pltpu.roll(second, BS, 1))
+                odd = jnp.where(low, pltpu.roll(first, BS, 1), second)
+                at = pair * 2 * half
+                out_ref[group, at : at + half, :] = even.astype(out_ref.dtype)
+                out_ref[group, at + half : at + 2 * half, :] = odd.astype(out_ref.dtype)
+        leaves[step].start()
+    for copy in leaves:
+        copy.wait()
 
 
 def reorder_tiles(bands):
-    groups, depth, _ = bands.shape
     steps = 4
-    block = pl.BlockSpec((groups // steps, depth, LANES), lambda i: (i, 0, 0))
+    anywhere = pl.BlockSpec(memory_space=pl.ANY)
     return pl.pallas_call(
         reorder_kernel,
-        grid=(steps,),
-        in_specs=[block],
-        out_specs=block,
+        in_specs=[anywhere],
+        out_specs=anywhere,
         out_shape=jax.ShapeDtypeStruct(bands.shape, bands.dtype),
-        scratch_shapes=[pltpu.VMEM((depth, depth), jnp.bfloat16)],
+        scratch_shapes=[
+            pltpu.VMEM(bands.shape, bands.dtype),
+            pltpu.VMEM(bands.shape, bands.dtype),
+            pltpu.SemaphoreType.DMA((steps,)),
+            pltpu.SemaphoreType.DMA((steps,)),
+        ],
+        compiler_params=pltpu.CompilerParams(vmem_limit_bytes=62 << 20),
         name="reorder_tiles",
     )(bands)
 
@@ -119,7 +130,6 @@
     refs = list(refs)
     index_hbm, in_ref, bias_ref = (refs.pop(0) for _ in range(3))
     given_ref = None if fetch else refs.pop(0)
-    sent_hbm = refs.pop(0) if kind == "first" else None
     weights_hbm = refs.pop(0) if fetch or ahead else None
     out_ref = refs.pop(0)
     next_ref = refs.pop(0) if ahead else None
@@ -140,13 +150,7 @@
         span = pl.ds(step * per_step, per_step)
         return pltpu.make_async_copy(source.at[span], fetched_ref.at[span], tile_sems.at[step])
 
-    if kind == "first":
-        core = lax.axis_index("section") % 2
-        tiles_hbm = weights_hbm
-        for step in range(steps):
-            pl.when(core == 0)(tile_copy(tiles_hbm, step).start)
-            pl.when(core == 1)(tile_copy(sent_hbm, step).start)
-    elif fetch:
+    if fetch:
         tiles_hbm = weights_hbm.at[layer]
         for step in range(steps):
             tile_copy(tiles_hbm, step).start()
@@ -212,12 +216,12 @@
                 out_ref[target, tile * chunk : (tile + 1) * chunk] = value[at : at + chunk]
 
 
-def run_layer(index, incoming, bias, layer, kind, blocks, layers, weights=None, given=None, sent=None):
+def run_layer(index, incoming, bias, layer, kind, blocks, layers, weights=None, given=None):
     shards, rows, _ = incoming.shape
     fetch = given is None
     ahead = kind == "inner"
     groups, depth = (weights if fetch else given).shape[-3:-1]
-    steps = 4
+    steps = 2
     if kind == "first":
         out_shape = (layers, rows // (layers // 2) * blocks // 2, LANES)
     elif kind == "last":
@@ -229,8 +233,6 @@
     operands = [(index, anywhere), (incoming, in_vmem), (bias, in_vmem)]
     if not fetch:
         operands.append((given, in_vmem))
-    if kind == "first":
-        operands.append((sent, anywhere))
     if fetch or ahead:
         operands.append((weights, anywhere))
     results = [jax.ShapeDtypeStruct(out_shape, jnp.bfloat16)]
@@ -286,8 +288,11 @@
     rank = jnp.concatenate(ranks, axis=0)
     slot = jnp.where(used, 2 * (own_rows // blocks_dev) + rank, 0)
     column = jnp.where(used, cols_ref[...], blocks_dev)
+    shards = counts_ref.shape[1]
+    shard_lane = lax.broadcasted_iota(jnp.int32, (LANES, shards), 1)
+    shard_sub = lax.broadcasted_iota(jnp.int32, (LANES, shards), 0) // per_shard
     counts = jnp.sum(
-        jnp.where(lane == sub // per_shard, jnp.broadcast_to(counts_ref[...], (LANES, LANES)), 0).astype(jnp.float32),
+        jnp.where(shard_lane == shard_sub, jnp.broadcast_to(counts_ref[...], (LANES, shards)), 0).astype(jnp.float32),
         axis=1,
         keepdims=True,
     ).astype(jnp.int32)
@@ -321,10 +326,8 @@
 
 
 def plan_routes(tile_row, tile_col, tile_count, bias, features, blocks_dev, layers):
-    shards = tile_count.shape[1]
     rows, width = features.shape
     in_vmem = pl.BlockSpec(memory_space=pltpu.VMEM)
-    counts = jnp.pad(tile_count, ((0, 0), (0, LANES - shards)))
     return pl.pallas_call(
         functools.partial(plan_kernel, blocks_dev),
         in_specs=[pl.BlockSpec(memory_space=pltpu.SMEM)] + [in_vmem] * 5,
@@ -336,7 +339,7 @@
         tile_count[0],
         tile_row.reshape(-1, LANES),
         tile_col.reshape(-1, LANES),
-        counts,
+        tile_count,
         bias.reshape(-1, LANES),
         features,
     )
@@ -365,9 +368,10 @@
         biases = jnp.pad(biases, ((0, 0), (0, 0), (0, LANES - BS)))
     with jax.named_scope("first_layer"):
         sent = lax.ppermute(ordered, "section", to_odd)
+        first_tiles = jnp.where(lax.axis_index("section") % 2 == 0, ordered, sent)
         outgoing = pack_rows(index, shared, 0, layers // 2, shards, rows * layers // 2, blocks)
         incoming = lax.all_to_all(outgoing, "neuron", 0, 0, tiled=True)
-        finished = run_layer(index, incoming, biases, 0, "first", blocks, layers, weights=ordered, sent=sent)
+        finished = run_layer(index, incoming, biases, 0, "first", blocks, layers, given=first_tiles)
         own_rows = lax.all_to_all(finished, "section", 0, 0, tiled=True)
     with jax.named_scope("layers"):
         outgoing = pack_rows(index, own_rows, 1, 1, shards, rows, blocks)

time: 248 us -> 247 us (level)
  Pallas kernels: 29.2 us -> 26.1 us
  blocking collectives: 145 us -> 148 us
    all_to_all x7, blocking collectives: 132 us -> 135 us  [body(): incoming = lax.all_to_all(outgoing, 'neuron', 0, 0, tiled=True)]
  transfers between devices with their start and end apart: 4 -> 4, of which waited for: 2 -> 2; matrix products, arithmetic and copies ran while one was open for 0% -> 1% of each run, Pallas kernels for 4% -> 3%
where the time goes in v4:
time: 247 us; the launch traced here: 246 us
  blocking collectives  148 us (60%)
  waiting for transfers between devices  31.5 us (13%)
  Pallas kernels  26.1 us (11%)
  starting transfers between devices  24.8 us (10%)
  between operations  13.5 us (5%)
    all_to_all x7, blocking collectives, body(): incoming = lax.all_to_all(outgoing, 'neuron', 0, 0, tiled=True)  135 us
    all_to_all x1, waiting for transfers between devices, body(): incoming = lax.all_to_all(outgoing, 'neuron', 0, 0, tiled=True)  27.6 us
    pallas_call x8, Pallas kernels, run_layer(): pl.pallas_call(functools.partial(layer_kernel, layer, kind, fetch, ahead)...  17.7 us
    all_to_all x1, blocking collectives, body(): own_rows = lax.all_to_all(finished, 'section', 0, 0, tiled=True)  13.1 us
    all_to_all x1, starting transfers between devices, body(): incoming = lax.all_to_all(outgoing, 'neuron', 0, 0, tiled=True)  12.1 us
    all_to_all x1, starting transfers between devices, body(): shared = lax.all_to_all(plan, 'section', 0, 0, tiled=True)  9.26 us
  transfers between devices with their start and end apart: 4, of which 2 were waited for; matrix products, arithmetic and copies ran while one was open for 1% of the time, Pallas kernels for 3%

profile of v4, /device:TPU:2, one launch (start us, length us, event | category | flops | bytes accessed | tf_op | source)
XLA Modules:
  0.0 246.0 jit_solution(12441271186065043278)
XLA Ops:
  6.5 0.0 all-gather.3.cloned.1.call-start
  6.5 3.9 %reorder_tiles.1 = bf16[32,256,128]{2,1,0:T(8,128)(2,1)} custom-call(bf16[32,256,128]{2,1,0:T(8,128)(2,1)} %bitcast.21), custom_call_target="tpu_custom_call" | custom-call | tf_op jit(solution)/shard_map/tile_order/reorder_tiles/pallas_call | solution.py:57
  10.4 0.0 all-gather.3.cloned.1.call-update
  10.5 2.0 plan_routes.1
  12.5 9.3 %all-to-all-start = ((bf16[8,176,128]{2,1,0:T(8,128)(2,1)}), bf16[8,176,128]{2,1,0:T(8,128)(2,1)S(1)}, u32[]{:S(2)}, u32[]{:S(2)}) async-start(bf16[8,176,128]{2,1,0:T(8,128)(2,1)} %plan_routes.1), calls=%async_computation | async-start | bytes 720896 | tf_op jit(solution)/shard_map/routes/all_to_all | solution.py:363
  21.7 3.4 %collective-permute-start = (bf16[32,256,128]{2,1,0:T(8,128)(2,1)}, bf16[32,256,128]{2,1,0:T(8,128)(2,1)}, u32[]{:S(2)}, u32[]{:S(2)}) collective-permute-start(bf16[32,256,128]{2,1,0:T(8,128)(2,1)} %reorder_tiles.1), channel_id=1, source_target_pairs={{0,64},{128,192},{256,320},{384,448},{1,65},{129,193},{257,321},{3... | collective-permute-start | bytes 6291464 | tf_op jit(solution)/shard_map/first_layer/ppermute | solution.py:370
  25.1 3.8 %all-to-all-done.in_ref = bf16[8,176,128]{2,1,0:T(8,128)(2,1)S(1)} async-done(((bf16[8,176,128]{2,1,0:T(8,128)(2,1)}), bf16[8,176,128]{2,1,0:T(8,128)(2,1)S(1)}, u32[]{:S(2)}, u32[]{:S(2)}) %all-to-all-start) | async-done | bytes 360480 | tf_op jit(solution)/shard_map/routes/all_to_all | solution.py:363
  28.9 1.8 pack_rows.2
  30.7 12.1 %all-to-all-start.1 = ((bf16[64,64,128]{2,1,0:T(8,128)(2,1)}), bf16[64,64,128]{2,1,0:T(8,128)(2,1)S(1)}, u32[]{:S(2)}, u32[]{:S(2)}) async-start(bf16[64,64,128]{2,1,0:T(8,128)(2,1)} %pack_rows.2), calls=%async_computation.1 | async-start | bytes 2097152 | tf_op jit(solution)/shard_map/first_layer/all_to_all | solution.py:373
  42.9 0.1 reshape.25
  43.0 0.0 collective-permute-done
  43.0 1.9 broadcast_select_fusion.refs_3_
  44.9 27.6 %all-to-all-done.1.refs_1_ = bf16[64,64,128]{2,1,0:T(8,128)(2,1)S(1)} async-done(((bf16[64,64,128]{2,1,0:T(8,128)(2,1)}), bf16[64,64,128]{2,1,0:T(8,128)(2,1)S(1)}, u32[]{:S(2)}, u32[]{:S(2)}) %all-to-all-start.1) | async-done | bytes 1048608 | tf_op jit(solution)/shard_map/first_layer/all_to_all | solution.py:373
  72.5 3.6 %layer_step.8 = bf16[8,128,128]{2,1,0:T(8,128)(2,1)S(1)} custom-call(s32[8192]{0:T(1024)S(1)} %fusion.index_hbm.refs_0_, bf16[64,64,128]{2,1,0:T(8,128)(2,1)S(1)} %all-to-all-done.1.refs_1_, f32[8,16,128]{2,1,0:T(8,128)S(1)} %pad.4.refs_2_, bf16[32,256,128]{2,1,0:T(8,128)(2,1)S(1)} %broadcast_select_fusion.refs_3_), custom_call_target="tpu_custom_call" | custom-call | flops 2147483648 | bytes 3145728 | tf_op jit(solution)/shard_map/first_layer/layer_step/pallas_call | solution.py:241
  76.1 13.1 %all_to_all.50.in_ref = bf16[8,128,128]{2,1,0:T(8,128)(2,1)S(1)} all-to-all(bf16[8,128,128]{2,1,0:T(8,128)(2,1)S(1)} %layer_step.8), channel_id=1, replica_groups=mesh['section'=8,'neuron'=64] {'section'}, dimensions={0} | all-to-all | bytes 524288 | tf_op jit(solution)/shard_map/first_layer/all_to_all | solution.py:375
  89.2 0.7 pack_rows.3
  90.0 20.9 %all_to_all.51.refs_1_ = bf16[64,16,128]{2,1,0:T(8,128)(2,1)S(1)} all-to-all(bf16[64,16,128]{2,1,0:T(8,128)(2,1)S(1)} %pack_rows.3), channel_id=1, replica_groups=mesh['section'=8,'neuron'=64] {'neuron'}, dimensions={0} | all-to-all | bytes 524288 | tf_op jit(solution)/shard_map/layers/all_to_all | solution.py:380
  110.8 0.0 all-gather.3.cloned.1.call-done
  110.8 2.6 %layer_step.9 = (bf16[64,16,128]{2,1,0:T(8,128)(2,1)S(1)}, bf16[32,256,128]{2,1,0:T(8,128)(2,1)S(1)}) custom-call(s32[8192]{0:T(1024)S(1)} %fusion.index_hbm.refs_0_, bf16[64,16,128]{2,1,0:T(8,128)(2,1)S(1)} %all_to_all.51.refs_1_, f32[8,16,128]{2,1,0:T(8,128)S(1)} %pad.4.refs_2_, bf16[8,32,256,128]{3,2,1,0:T(8,128)(2,1)} %bitcast.15), custom_call_target="tpu_custom_call" | custom-call | flops 536870912 | bytes 3145728 | tf_op jit(solution)/shard_map/layers/layer_step/pallas_call | solution.py:241
  113.5 25.6 %all_to_all.52.refs_1_ = bf16[64,16,128]{2,1,0:T(8,128)(2,1)S(1)} all-to-all(bf16[64,16,128]{2,1,0:T(8,128)(2,1)S(1)} %get-tuple-element.17), channel_id=1, replica_groups=mesh['section'=8,'neuron'=64] {'neuron'}, dimensions={0} | all-to-all | bytes 524288 | tf_op jit(solution)/shard_map/layers/all_to_all | solution.py:380
  139.1 1.9 layer_step.10
  140.9 18.3 %all_to_all.53.refs_1_ = bf16[64,16,128]{2,1,0:T(8,128)(2,1)S(1)} all-to-all(bf16[64,16,128]{2,1,0:T(8,128)(2,1)S(1)} %get-tuple-element.19), channel_id=1, replica_groups=mesh['section'=8,'neuron'=64] {'neuron'}, dimensions={0} | all-to-all | bytes 524288 | tf_op jit(solution)/shard_map/layers/all_to_all | solution.py:380
  159.2 1.9 layer_step.11
  161.1 17.9 %all_to_all.54.refs_1_ = bf16[64,16,128]{2,1,0:T(8,128)(2,1)S(1)} all-to-all(bf16[64,16,128]{2,1,0:T(8,128)(2,1)S(1)} %get-tuple-element.21), channel_id=1, replica_groups=mesh['section'=8,'neuron'=64] {'neuron'}, dimensions={0} | all-to-all | bytes 524288 | tf_op jit(solution)/shard_map/layers/all_to_all | solution.py:380
  179.1 1.8 layer_step.12
  180.9 17.5 %all_to_all.55.refs_1_ = bf16[64,16,128]{2,1,0:T(8,128)(2,1)S(1)} all-to-all(bf16[64,16,128]{2,1,0:T(8,128)(2,1)S(1)} %get-tuple-element.23), channel_id=1, replica_groups=mesh['section'=8,'neuron'=64] {'neuron'}, dimensions={0} | all-to-all | bytes 524288 | tf_op jit(solution)/shard_map/layers/all_to_all | solution.py:380
  198.4 1.8 layer_step.13
  200.3 17.4 %all_to_all.56.refs_1_ = bf16[64,16,128]{2,1,0:T(8,128)(2,1)S(1)} all-to-all(bf16[64,16,128]{2,1,0:T(8,128)(2,1)S(1)} %get-tuple-element.25), channel_id=1, replica_groups=mesh['section'=8,'neuron'=64] {'neuron'}, dimensions={0} | all-to-all | bytes 524288 | tf_op jit(solution)/shard_map/layers/all_to_all | solution.py:380
  217.7 1.8 layer_step.14
  219.5 17.4 %all_to_all.57.refs_1_ = bf16[64,16,128]{2,1,0:T(8,128)(2,1)S(1)} all-to-all(bf16[64,16,128]{2,1,0:T(8,128)(2,1)S(1)} %get-tuple-element.27), channel_id=1, replica_groups=mesh['section'=8,'neuron'=64] {'neuron'}, dimensions={0} | all-to-all | bytes 524288 | tf_op jit(solution)/shard_map/layers/all_to_all | solution.py:382
  236.9 2.2 layer_step.15
  (3 shorter events, 0.0 us)
Async XLA Ops:
  6.5 104.3 %all-gather.3.cloned.1.call-start = ((), (), s32[]{:S(2)}) async-start(), calls=%async_computation.10 | async-start | bytes 18874368 | tf_op jit(solution)/shard_map/weight_gather/all_gather | solution.py:360
  12.5 16.4 %all-to-all-start = ((bf16[8,176,128]{2,1,0:T(8,128)(2,1)}), bf16[8,176,128]{2,1,0:T(8,128)(2,1)S(1)}, u32[]{:S(2)}, u32[]{:S(2)}) async-start(bf16[8,176,128]{2,1,0:T(8,128)(2,1)} %plan_routes.1), calls=%async_computation | async-start | bytes 720896 | tf_op jit(solution)/shard_map/routes/all_to_all | solution.py:363
  21.7 21.3 %collective-permute-start = (bf16[32,256,128]{2,1,0:T(8,128)(2,1)}, bf16[32,256,128]{2,1,0:T(8,128)(2,1)}, u32[]{:S(2)}, u32[]{:S(2)}) collective-permute-start(bf16[32,256,128]{2,1,0:T(8,128)(2,1)} %reorder_tiles.1), channel_id=1, source_target_pairs={{0,64},{128,192},{256,320},{384,448},{1,65},{129,193},{257,321},{3... | collective-permute-start | bytes 6291464 | tf_op jit(solution)/shard_map/first_layer/ppermute | solution.py:370
  30.7 41.8 %all-to-all-start.1 = ((bf16[64,64,128]{2,1,0:T(8,128)(2,1)}), bf16[64,64,128]{2,1,0:T(8,128)(2,1)S(1)}, u32[]{:S(2)}, u32[]{:S(2)}) async-start(bf16[64,64,128]{2,1,0:T(8,128)(2,1)} %pack_rows.2), calls=%async_computation.1 | async-start | bytes 2097152 | tf_op jit(solution)/shard_map/first_layer/all_to_all | solution.py:373
Sparse Core Ops, SparseCore 0:
  10.6 97.3 all-gather.2

commit v5 on v4

--- a/solution.py
+++ b/solution.py
@@ -91,15 +91,21 @@
         out_ref[shard] = low_ref[first] + high_ref[second]
 
 
-def pack_kernel(at, sources, index_hbm, in_ref, out_ref, index_ref, low_ref, high_ref, index_sem):
+def pack_kernel(at, sources, index_hbm, *refs):
+    *in_refs, out_ref, index_ref, low_ref, high_ref, index_sem = refs
     chunk = out_ref.shape[1] // sources
     index_copy = pltpu.make_async_copy(index_hbm.at[pl.ds(at * INDEX_STRIDE, INDEX_STRIDE)], index_ref, index_sem)
     index_copy.start()
-    core = lax.axis_index("section") % 2
+    section = lax.axis_index("section")
     matrices = [spread_matrix(offset * BS) for offset in range(2)]
     for tile in range(low_ref.shape[0] // 2):
         span = pl.ds(tile * chunk, chunk)
-        value = jnp.concatenate([in_ref[2 * source + core, span] for source in range(sources)], axis=0)
+        if sources == 1:
+            value = in_refs[0][span]
+            for chip in range(1, len(in_refs)):
+                value = jnp.where(section // 2 == chip, in_refs[chip][span], value)
+        else:
+            value = jnp.concatenate([in_refs[0][2 * source + section % 2, span] for source in range(sources)], axis=0)
         for offset in range(2):
             spread = jnp.dot(value, matrices[offset], preferred_element_type=jnp.float32).astype(jnp.bfloat16)
             low_ref[2 * tile + offset] = spread[:, :LANES]
@@ -108,11 +114,11 @@
     pack_blocks(index_ref, PICKS_AT, low_ref, high_ref, out_ref)
 
 
-def pack_rows(index, rows_in, at, sources, shards, rows, blocks):
+def pack_rows(index, arrays, at, sources, shards, rows, blocks):
     in_vmem = pl.BlockSpec(memory_space=pltpu.VMEM)
     return pl.pallas_call(
         functools.partial(pack_kernel, at, sources),
-        in_specs=[pl.BlockSpec(memory_space=pl.ANY), in_vmem],
+        in_specs=[pl.BlockSpec(memory_space=pl.ANY)] + [in_vmem] * len(arrays),
         out_specs=in_vmem,
         scratch_shapes=[
             pltpu.SMEM((INDEX_STRIDE,), jnp.int32),
@@ -123,7 +129,7 @@
         out_shape=jax.ShapeDtypeStruct((shards, rows, LANES), jnp.bfloat16),
         compiler_params=pltpu.CompilerParams(vmem_limit_bytes=VMEM_LIMIT),
         name="pack_rows",
-    )(index, rows_in)
+    )(index, *arrays)
 
 
 def layer_kernel(layer, kind, fetch, ahead, *refs):
@@ -131,7 +137,8 @@
     index_hbm, in_ref, bias_ref = (refs.pop(0) for _ in range(3))
     given_ref = None if fetch else refs.pop(0)
     weights_hbm = refs.pop(0) if fetch or ahead else None
-    out_ref = refs.pop(0)
+    out_refs = [refs.pop(0) for _ in range(lax.axis_size("section") // 2 if kind == "first" else 1)]
+    out_ref = out_refs[0]
     next_ref = refs.pop(0) if ahead else None
     index_ref, fetched_ref, spread_ref, low_ref, high_ref, index_sem, tile_sems, next_sem, *total_refs = refs
     tiles_ref = fetched_ref if fetch else given_ref
@@ -210,10 +217,9 @@
         if kind == "last":
             out_ref[:, tile * LANES : (tile + 1) * LANES] = value
         else:
-            chunk = out_ref.shape[1] // (blocks // 2)
-            for target in range(out_ref.shape[0]):
-                at = target // 2 * chunk
-                out_ref[target, tile * chunk : (tile + 1) * chunk] = value[at : at + chunk]
+            chunk = rows // len(out_refs)
+            for chip, chip_ref in enumerate(out_refs):
+                chip_ref[tile * chunk : (tile + 1) * chunk] = value[chip * chunk : (chip + 1) * chunk]
 
 
 def run_layer(index, incoming, bias, layer, kind, blocks, layers, weights=None, given=None):
@@ -223,7 +229,7 @@
     groups, depth = (weights if fetch else given).shape[-3:-1]
     steps = 2
     if kind == "first":
-        out_shape = (layers, rows // (layers // 2) * blocks // 2, LANES)
+        out_shape = (rows // (layers // 2) * blocks // 2, LANES)
     elif kind == "last":
         out_shape = (rows, blocks * BS)
     else:
@@ -235,7 +241,7 @@
         operands.append((given, in_vmem))
     if fetch or ahead:
         operands.append((weights, anywhere))
-    results = [jax.ShapeDtypeStruct(out_shape, jnp.bfloat16)]
+    results = [jax.ShapeDtypeStruct(out_shape, jnp.bfloat16)] * (layers // 2 if kind == "first" else 1)
     if ahead:
         results.append(jax.ShapeDtypeStruct((groups, depth, LANES), jnp.bfloat16))
     done = pl.pallas_call(
@@ -258,7 +264,7 @@
         cost_estimate=pl.CostEstimate(flops=2 * groups * GROUP * 2 * rows * depth * LANES, bytes_accessed=3 << 20, transcendentals=0),
         name="layer_step",
     )(*[operand for operand, _ in operands])
-    return done if ahead else done[0]
+    return done if len(results) > 1 else done[0]
 
 
 def plan_kernel(blocks_dev, count_ref, rows_ref, cols_ref, counts_ref, bias_ref, in_ref, out_ref):
@@ -369,10 +375,13 @@
     with jax.named_scope("first_layer"):
         sent = lax.ppermute(ordered, "section", to_odd)
         first_tiles = jnp.where(lax.axis_index("section") % 2 == 0, ordered, sent)
-        outgoing = pack_rows(index, shared, 0, layers // 2, shards, rows * layers // 2, blocks)
+        outgoing = pack_rows(index, [shared], 0, layers // 2, shards, rows * layers // 2, blocks)
         incoming = lax.all_to_all(outgoing, "neuron", 0, 0, tiled=True)
         finished = run_layer(index, incoming, biases, 0, "first", blocks, layers, given=first_tiles)
-        own_rows = lax.all_to_all(finished, "section", 0, 0, tiled=True)
+        own_rows = [finished[0]] + [
+            lax.ppermute(finished[chip], "section", [(core, 2 * chip + core) for core in range(2)])
+            for chip in range(1, layers // 2)
+        ]
     with jax.named_scope("layers"):
         outgoing = pack_rows(index, own_rows, 1, 1, shards, rows, blocks)
         given = None

time: 247 us -> 244 us (0.988)
  blocking collectives: 148 us -> 137 us
  waiting for transfers between devices: 31.5 us -> 37.2 us
  starting transfers between devices: 24.8 us -> 27.4 us
    all_to_all x1 -> x0, blocking collectives: 13.1 us -> none  [body(): own_rows = lax.all_to_all(finished, 'section', 0, 0, tiled=True)]
    ppermute x0 -> x3, waiting for transfers between devices: none -> 3.84 us  [body(): lax.ppermute(finished[chip], 'section', [(core, 2 * chip + core) for core...]
    ppermute x0 -> x3, starting transfers between devices: none -> 2.62 us  [body(): lax.ppermute(finished[chip], 'section', [(core, 2 * chip + core) for core...]
  transfers between devices with their start and end apart: 4 -> 7, of which waited for: 2 -> 4; matrix products, arithmetic and copies ran while one was open for 1% -> 1% of each run, Pallas kernels for 3% -> 3%
where the time goes in v5:
time: 244 us; the launch traced here: 243 us
  blocking collectives  137 us (56%)
  waiting for transfers between devices  37.2 us (15%)
  starting transfers between devices  27.4 us (11%)
  Pallas kernels  26.1 us (11%)
  between operations  13.6 us (6%)
    all_to_all x7, blocking collectives, body(): incoming = lax.all_to_all(outgoing, 'neuron', 0, 0, tiled=True)  137 us
    all_to_all x1, waiting for transfers between devices, body(): incoming = lax.all_to_all(outgoing, 'neuron', 0, 0, tiled=True)  27.6 us
    pallas_call x8, Pallas kernels, run_layer(): pl.pallas_call(functools.partial(layer_kernel, layer, kind, fetch, ahead)...  17.6 us
    all_to_all x1, starting transfers between devices, body(): incoming = lax.all_to_all(outgoing, 'neuron', 0, 0, tiled=True)  12.1 us
    all_to_all x1, starting transfers between devices, body(): shared = lax.all_to_all(plan, 'section', 0, 0, tiled=True)  9.26 us
  transfers between devices with their start and end apart: 7, of which 4 were waited for; matrix products, arithmetic and copies ran while one was open for 1% of the time, Pallas kernels for 3%

profile of v5, /device:TPU:2, one launch (start us, length us, event | category | flops | bytes accessed | tf_op | source)
XLA Modules:
  0.0 243.2 jit_solution(3410315881918315687)
XLA Ops:
  6.5 0.0 all-gather.3.cloned.1.call-start
  6.5 3.9 %reorder_tiles.1 = bf16[32,256,128]{2,1,0:T(8,128)(2,1)} custom-call(bf16[32,256,128]{2,1,0:T(8,128)(2,1)} %bitcast.21), custom_call_target="tpu_custom_call" | custom-call | tf_op jit(solution)/shard_map/tile_order/reorder_tiles/pallas_call | solution.py:57
  10.5 0.0 all-gather.3.cloned.1.call-update
  10.5 2.0 plan_routes.1
  12.5 9.3 %all-to-all-start = ((bf16[8,176,128]{2,1,0:T(8,128)(2,1)}), bf16[8,176,128]{2,1,0:T(8,128)(2,1)S(1)}, u32[]{:S(2)}, u32[]{:S(2)}) async-start(bf16[8,176,128]{2,1,0:T(8,128)(2,1)} %plan_routes.1), calls=%async_computation | async-start | bytes 720896 | tf_op jit(solution)/shard_map/routes/all_to_all | solution.py:369
  21.8 3.4 %collective-permute-start = (bf16[32,256,128]{2,1,0:T(8,128)(2,1)}, bf16[32,256,128]{2,1,0:T(8,128)(2,1)}, u32[]{:S(2)}, u32[]{:S(2)}) collective-permute-start(bf16[32,256,128]{2,1,0:T(8,128)(2,1)} %reorder_tiles.1), channel_id=1, source_target_pairs={{0,64},{128,192},{256,320},{384,448},{1,65},{129,193},{257,321},{3... | collective-permute-start | bytes 6291464 | tf_op jit(solution)/shard_map/first_layer/ppermute | solution.py:376
  25.1 3.8 %all-to-all-done.refs_0_ = bf16[8,176,128]{2,1,0:T(8,128)(2,1)S(1)} async-done(((bf16[8,176,128]{2,1,0:T(8,128)(2,1)}), bf16[8,176,128]{2,1,0:T(8,128)(2,1)S(1)}, u32[]{:S(2)}, u32[]{:S(2)}) %all-to-all-start) | async-done | bytes 360480 | tf_op jit(solution)/shard_map/routes/all_to_all | solution.py:369
  28.9 1.8 pack_rows.2
  30.8 12.1 %all-to-all-start.1 = ((bf16[64,64,128]{2,1,0:T(8,128)(2,1)}), bf16[64,64,128]{2,1,0:T(8,128)(2,1)S(1)}, u32[]{:S(2)}, u32[]{:S(2)}) async-start(bf16[64,64,128]{2,1,0:T(8,128)(2,1)} %pack_rows.2), calls=%async_computation.1 | async-start | bytes 2097152 | tf_op jit(solution)/shard_map/first_layer/all_to_all | solution.py:379
  43.0 0.1 reshape.25
  43.1 0.0 collective-permute-done
  43.1 1.9 broadcast_select_fusion.refs_3_
  44.9 27.6 %all-to-all-done.1.refs_1_ = bf16[64,64,128]{2,1,0:T(8,128)(2,1)S(1)} async-done(((bf16[64,64,128]{2,1,0:T(8,128)(2,1)}), bf16[64,64,128]{2,1,0:T(8,128)(2,1)S(1)}, u32[]{:S(2)}, u32[]{:S(2)}) %all-to-all-start.1) | async-done | bytes 1048608 | tf_op jit(solution)/shard_map/first_layer/all_to_all | solution.py:379
  72.6 3.6 %layer_step.8 = (bf16[128,128]{1,0:T(8,128)(2,1)S(1)}, bf16[128,128]{1,0:T(8,128)(2,1)S(1)}, bf16[128,128]{1,0:T(8,128)(2,1)S(1)}, bf16[128,128]{1,0:T(8,128)(2,1)S(1)}) custom-call(s32[8192]{0:T(1024)S(1)} %fusion.index_hbm.refs_0_, bf16[64,64,128]{2,1,0:T(8,128)(2,1)S(1)} %all-to-all-done.1.refs_1_, f32[8,16,128]{2,1,0:T(8,128)S(1)} %pad.4.refs_2_, ...), custom_call_target="tpu_custom_call" | custom-call | flops 2147483648 | bytes 3145728 | tf_op jit(solution)/shard_map/first_layer/layer_step/pallas_call | solution.py:247
  76.2 1.3 collective-permute-start.1
  77.5 0.7 collective-permute-start.2
  78.1 0.7 collective-permute-start.3
  78.8 3.8 %collective-permute-done.1.refs_1_ = bf16[128,128]{1,0:T(8,128)(2,1)S(1)} collective-permute-done((bf16[128,128]{1,0:T(8,128)(2,1)S(1)}, bf16[128,128]{1,0:T(8,128)(2,1)S(1)}, u32[]{:S(2)}, u32[]{:S(2)}) %collective-permute-start.1) | collective-permute-done | bytes 32800 | tf_op jit(solution)/shard_map/first_layer/ppermute | solution.py:382
  82.6 0.0 collective-permute-done.2.refs_2_
  82.7 0.0 collective-permute-done.3.refs_3_
  82.7 0.7 pack_rows.3
  83.4 19.9 %all_to_all.45.refs_1_ = bf16[64,16,128]{2,1,0:T(8,128)(2,1)S(1)} all-to-all(bf16[64,16,128]{2,1,0:T(8,128)(2,1)S(1)} %pack_rows.3), channel_id=1, replica_groups=mesh['section'=8,'neuron'=64] {'neuron'}, dimensions={0} | all-to-all | bytes 524288 | tf_op jit(solution)/shard_map/layers/all_to_all | solution.py:389
  103.3 1.9 all-gather.3.cloned.1.call-done
  105.2 2.6 %layer_step.9 = (bf16[64,16,128]{2,1,0:T(8,128)(2,1)S(1)}, bf16[32,256,128]{2,1,0:T(8,128)(2,1)S(1)}) custom-call(s32[8192]{0:T(1024)S(1)} %fusion.index_hbm.refs_0_, bf16[64,16,128]{2,1,0:T(8,128)(2,1)S(1)} %all_to_all.45.refs_1_, f32[8,16,128]{2,1,0:T(8,128)S(1)} %pad.4.refs_2_, bf16[8,32,256,128]{3,2,1,0:T(8,128)(2,1)} %bitcast.15), custom_call_target="tpu_custom_call" | custom-call | flops 536870912 | bytes 3145728 | tf_op jit(solution)/shard_map/layers/layer_step/pallas_call | solution.py:247
  107.8 28.4 %all_to_all.46.refs_1_ = bf16[64,16,128]{2,1,0:T(8,128)(2,1)S(1)} all-to-all(bf16[64,16,128]{2,1,0:T(8,128)(2,1)S(1)} %get-tuple-element.25), channel_id=1, replica_groups=mesh['section'=8,'neuron'=64] {'neuron'}, dimensions={0} | all-to-all | bytes 524288 | tf_op jit(solution)/shard_map/layers/all_to_all | solution.py:389
  136.3 1.8 layer_step.10
  138.1 18.4 %all_to_all.47.refs_1_ = bf16[64,16,128]{2,1,0:T(8,128)(2,1)S(1)} all-to-all(bf16[64,16,128]{2,1,0:T(8,128)(2,1)S(1)} %get-tuple-element.27), channel_id=1, replica_groups=mesh['section'=8,'neuron'=64] {'neuron'}, dimensions={0} | all-to-all | bytes 524288 | tf_op jit(solution)/shard_map/layers/all_to_all | solution.py:389
  156.4 1.8 layer_step.11
  158.3 17.9 %all_to_all.48.refs_1_ = bf16[64,16,128]{2,1,0:T(8,128)(2,1)S(1)} all-to-all(bf16[64,16,128]{2,1,0:T(8,128)(2,1)S(1)} %get-tuple-element.29), channel_id=1, replica_groups=mesh['section'=8,'neuron'=64] {'neuron'}, dimensions={0} | all-to-all | bytes 524288 | tf_op jit(solution)/shard_map/layers/all_to_all | solution.py:389
  176.2 1.9 layer_step.12
  178.0 17.6 %all_to_all.49.refs_1_ = bf16[64,16,128]{2,1,0:T(8,128)(2,1)S(1)} all-to-all(bf16[64,16,128]{2,1,0:T(8,128)(2,1)S(1)} %get-tuple-element.31), channel_id=1, replica_groups=mesh['section'=8,'neuron'=64] {'neuron'}, dimensions={0} | all-to-all | bytes 524288 | tf_op jit(solution)/shard_map/layers/all_to_all | solution.py:389
  195.7 1.8 layer_step.13
  197.5 17.4 %all_to_all.50.refs_1_ = bf16[64,16,128]{2,1,0:T(8,128)(2,1)S(1)} all-to-all(bf16[64,16,128]{2,1,0:T(8,128)(2,1)S(1)} %get-tuple-element.33), channel_id=1, replica_groups=mesh['section'=8,'neuron'=64] {'neuron'}, dimensions={0} | all-to-all | bytes 524288 | tf_op jit(solution)/shard_map/layers/all_to_all | solution.py:389
  214.9 1.8 layer_step.14
  216.7 17.4 %all_to_all.51.refs_1_ = bf16[64,16,128]{2,1,0:T(8,128)(2,1)S(1)} all-to-all(bf16[64,16,128]{2,1,0:T(8,128)(2,1)S(1)} %get-tuple-element.35), channel_id=1, replica_groups=mesh['section'=8,'neuron'=64] {'neuron'}, dimensions={0} | all-to-all | bytes 524288 | tf_op jit(solution)/shard_map/layers/all_to_all | solution.py:391
  234.1 2.2 layer_step.15
  (3 shorter events, 0.0 us)
Async XLA Ops:
  6.5 98.7 %all-gather.3.cloned.1.call-start = ((), (), s32[]{:S(2)}) async-start(), calls=%async_computation.9 | async-start | bytes 18874368 | tf_op jit(solution)/shard_map/weight_gather/all_gather | solution.py:366
  12.5 16.4 %all-to-all-start = ((bf16[8,176,128]{2,1,0:T(8,128)(2,1)}), bf16[8,176,128]{2,1,0:T(8,128)(2,1)S(1)}, u32[]{:S(2)}, u32[]{:S(2)}) async-start(bf16[8,176,128]{2,1,0:T(8,128)(2,1)} %plan_routes.1), calls=%async_computation | async-start | bytes 720896 | tf_op jit(solution)/shard_map/routes/all_to_all | solution.py:369
  21.8 21.3 %collective-permute-start = (bf16[32,256,128]{2,1,0:T(8,128)(2,1)}, bf16[32,256,128]{2,1,0:T(8,128)(2,1)}, u32[]{:S(2)}, u32[]{:S(2)}) collective-permute-start(bf16[32,256,128]{2,1,0:T(8,128)(2,1)} %reorder_tiles.1), channel_id=1, source_target_pairs={{0,64},{128,192},{256,320},{384,448},{1,65},{129,193},{257,321},{3... | collective-permute-start | bytes 6291464 | tf_op jit(solution)/shard_map/first_layer/ppermute | solution.py:376
  30.8 41.8 %all-to-all-start.1 = ((bf16[64,64,128]{2,1,0:T(8,128)(2,1)}), bf16[64,64,128]{2,1,0:T(8,128)(2,1)S(1)}, u32[]{:S(2)}, u32[]{:S(2)}) async-start(bf16[64,64,128]{2,1,0:T(8,128)(2,1)} %pack_rows.2), calls=%async_computation.1 | async-start | bytes 2097152 | tf_op jit(solution)/shard_map/first_layer/all_to_all | solution.py:379
  76.2 6.5 %collective-permute-start.1 = (bf16[128,128]{1,0:T(8,128)(2,1)S(1)}, bf16[128,128]{1,0:T(8,128)(2,1)S(1)}, u32[]{:S(2)}, u32[]{:S(2)}) collective-permute-start(bf16[128,128]{1,0:T(8,128)(2,1)S(1)} %get-tuple-element.22), channel_id=1, source_target_pairs={{0,128},{64,192},{1,129},{65,193},{2,130},{66,194},{3,131},{67,195... | collective-permute-start | bytes 98312 | tf_op jit(solution)/shard_map/first_layer/ppermute | solution.py:382
  77.5 5.2 %collective-permute-start.2 = (bf16[128,128]{1,0:T(8,128)(2,1)S(1)}, bf16[128,128]{1,0:T(8,128)(2,1)S(1)}, u32[]{:S(2)}, u32[]{:S(2)}) collective-permute-start(bf16[128,128]{1,0:T(8,128)(2,1)S(1)} %get-tuple-element.23), channel_id=1, source_target_pairs={{0,256},{64,320},{1,257},{65,321},{2,258},{66,322},{3,259},{67,323... | collective-permute-start | bytes 98312 | tf_op jit(solution)/shard_map/first_layer/ppermute | solution.py:382
  78.1 4.5 %collective-permute-start.3 = (bf16[128,128]{1,0:T(8,128)(2,1)S(1)}, bf16[128,128]{1,0:T(8,128)(2,1)S(1)}, u32[]{:S(2)}, u32[]{:S(2)}) collective-permute-start(bf16[128,128]{1,0:T(8,128)(2,1)S(1)} %get-tuple-element.24), channel_id=1, source_target_pairs={{0,384},{64,448},{1,385},{65,449},{2,386},{66,450},{3,387},{67,451... | collective-permute-start | bytes 98312 | tf_op jit(solution)/shard_map/first_layer/ppermute | solution.py:382
Sparse Core Ops, SparseCore 0:
  10.6 94.5 all-gather.2
